TPU v7x, 32 devices: a whole 2x2x4 slice. The times are simulated.
32 devices in a mesh: dp: 8 (over z, x), vocab: 4 (over y, core).
Axes of the slice: x: 2, y: 2, z: 4, core: 2. Of those that a mesh axis runs over, the one named last changes fastest.
Arguments:
- input_token_ids: int32 [2, 32, 512], P(None, ('dp', 'vocab')), may hold values from 0 to 50303
- lengths: int32 [2, 32], P(None, ('dp', 'vocab')), may hold values from 2 to 512, as said below
- masked_positions: int32 [2, 32, 76], P(None, ('dp', 'vocab')), may hold values from 1 to 511, as said below
- masked_token_targets: int32 [2, 32, 76], P(None, ('dp', 'vocab')), may hold values from 0 to 50303
- labels: int32 [2, 32], P(None, ('dp', 'vocab')), may hold values from 0 to 2
- token_embedding_table: bfloat16 [50304, 768], P('vocab'), may hold values from -0.649519 to 0.649519
- position_table: bfloat16 [512, 768], replicated, may hold values from -0.25 to 0.25
- norm_gain_table: float32 [6, 768], replicated, may hold values from 0.5 to 1.5
- query_key_value_weight: bfloat16 [2, 768, 2304], replicated, may hold values from -0.21875 to 0.21875
- output_weight: bfloat16 [2, 768, 768], replicated, may hold values from -0.875 to 0.875
- up_weight: bfloat16 [2, 768, 3072], replicated, may hold values from -0.21875 to 0.21875
- down_weight: bfloat16 [2, 3072, 768], replicated, may hold values from -0.109375 to 0.109375
- adapter_inputs: bfloat16 [2, 768, 40], replicated, may hold values from -0.21875 to 0.21875
- adapter_down_input: bfloat16 [2, 3072, 8], replicated, may hold values from -0.109375 to 0.109375
- head_dense_maps: bfloat16 [2, 768, 768], replicated, may hold values from -0.21875 to 0.21875
- adapter_outputs: float32 [2, 8, 6912], replicated, may hold values from -0.3125 to 0.3125
- class_projection: float32 [769, 3], replicated, may hold values from -0.21875 to 0.21875
- adapter_moment_first: float32 [2, 8, 6912], replicated, may hold values from -4.7683716e-06 to 4.7683716e-06
- adapter_moment_second: float32 [2, 8, 6912], replicated, may hold values from 8.857474e-15 to 3.5429897e-14
- class_moment_first: float32 [769, 3], replicated, may hold values from -4.7683716e-06 to 4.7683716e-06
- class_moment_second: float32 [769, 3], replicated, may hold values from 8.857474e-15 to 3.5429897e-14
Outputs:
- loss_and_terms: float32 [2], replicated
- grad_norm: float32 [1], replicated
- adapter_outputs_next: float32 [2, 8, 6912], replicated
- adapter_moment_first_next: float32 [2, 8, 6912], replicated
- adapter_moment_second_next: float32 [2, 8, 6912], replicated
- class_projection_next: float32 [769, 3], replicated
- class_moment_first_next: float32 [769, 3], replicated
- class_moment_second_next: float32 [769, 3], replicated
Inputs may be any that keep to these rules, and one draw needn't show every extreme that they name: `lengths`: some item of each micro-batch has length exactly 512. `masked_positions`: each position lies from 1 to its item's length minus 1; positions may repeat.
All inputs are finite; a program needn't handle non-finite values.
Results may differ from a plain program's by a relative error of at most 0.006.
Values may be sent and summed in bfloat16 or wider, within the bound.
No kernel may reach another device: no remote copies, remote signals or barrier semaphores. Data moves between devices by JAX's collectives and lax.ppermute only.
A program may use at most 320 MiB of HBM per device.

v0:
```python
import jax
import jax.numpy as jnp
from jax import lax
from jax.sharding import PartitionSpec as P

HDIM = 64
STEP = 10


FULL_PRECISION = lax.Precision.HIGHEST
NORM_EPS = 1e-05
ADAPTER_SCALE = 2.0
NEG_FILL = -1e30
CLIP_AT = 0.001
RATE = 0.03
BETA_ONE = 0.9
BETA_TWO = 0.999
ADAM_EPS = 1e-08
DECAY = 0.01


def layer_norm(values, gain):
    center = values - jnp.mean(values, -1, keepdims=True)
    spread = jnp.mean(center * center, -1, keepdims=True)
    return center * lax.rsqrt(spread + NORM_EPS) * gain


def half_precision_product(left, right):
    return jnp.dot(left, right, preferred_element_type=jnp.float32)


def dot_trans(left, right):
    return lax.dot_general(
        left, right, (((1,), (1,)), ((), ())), preferred_element_type=jnp.float32
    )


def precise_product(left, right):
    return jnp.dot(left, right, precision=FULL_PRECISION)


def inner_rows_low(rows, a_columns):
    return half_precision_product(rows, a_columns).astype(jnp.bfloat16)


def adapter_change(inner_low, adapter_out_columns, term_tally):
    row_tally = inner_low.shape[0]
    rank_size = adapter_out_columns.shape[0]
    output_width = adapter_out_columns.shape[1] // term_tally
    block_list = inner_low.astype(jnp.float32).reshape(row_tally, term_tally, rank_size)
    adapter_out_blocks = adapter_out_columns.reshape(rank_size, term_tally, output_width)
    return ADAPTER_SCALE * jnp.einsum(
        "bhx,xhs->bhs", block_list, adapter_out_blocks, precision=FULL_PRECISION
    ).reshape(row_tally, term_tally * output_width)


def adapter_backward(inner_low, grad_low, adapter_out_columns, adapter_in_columns, term_tally):
    row_tally = inner_low.shape[0]
    rank_size = adapter_out_columns.shape[0]
    output_width = adapter_out_columns.shape[1] // term_tally
    grad_blocks = grad_low.reshape(row_tally, term_tally, output_width)
    adapter_out_blocks = adapter_out_columns.reshape(rank_size, term_tally, output_width)
    adapter_out_gradient = ADAPTER_SCALE * jnp.einsum(
        "tjr,tjw->rjw",
        inner_low.reshape(row_tally, term_tally, rank_size),
        grad_blocks,
        preferred_element_type=jnp.float32,
    ).reshape(rank_size, term_tally * output_width)
    inner_gradient = ADAPTER_SCALE * jnp.einsum(
        "tjw,rjw->tjr",
        grad_blocks.astype(jnp.float32),
        adapter_out_blocks,
        precision=FULL_PRECISION,
    ).reshape(row_tally, term_tally * rank_size)
    return (
        dot_trans(inner_gradient.astype(jnp.bfloat16), adapter_in_columns),
        adapter_out_gradient,
    )


def norm_back(values, gain, grad):
    unused_out, backward_pull = jax.vjp(lambda inner_values: layer_norm(inner_values, gain), values)
    return backward_pull(grad)[0]


def attention_scores(qkv_low, key_valid_mask, item_count, seq_len, head_count):
    triple = qkv_low.reshape(item_count, seq_len, 3, head_count, HDIM)
    scores = jnp.einsum(
        "iqhd,ikhd->ihqk", triple[:, :, 0], triple[:, :, 1], preferred_element_type=jnp.float32
    )
    scores = jnp.where(key_valid_mask[:, None, None, :], scores * HDIM ** (-0.5), NEG_FILL)
    return (triple, scores)


def layer_forward(hidden_rows, params, key_valid_mask, item_count, seq_len):
    (
        query_key_value_weight,
        output_weight,
        up_weight,
        down_weight,
        a_in,
        a_down,
        adapter_out_columns,
        gain_pair,
    ) = params
    hidden_width = hidden_rows.shape[1]
    rank_size = a_down.shape[1]
    head_count = hidden_width // HDIM
    flattened_input = hidden_rows.astype(jnp.bfloat16)
    inner_attention_rows = inner_rows_low(flattened_input, a_in[:, : 3 * rank_size])
    qkv_low = (
        half_precision_product(flattened_input, query_key_value_weight)
        + adapter_change(inner_attention_rows, adapter_out_columns[:, : 3 * hidden_width], 3)
    ).astype(jnp.bfloat16)
    triple, scores = attention_scores(qkv_low, key_valid_mask, item_count, seq_len, head_count)
    row_top = jnp.max(scores, -1, keepdims=True)
    exponent = jnp.exp(scores - row_top)
    row_total = jnp.sum(exponent, -1, keepdims=True)
    probs = exponent / row_total
    log_total = row_top + jnp.log(row_total)
    attended_rows = jnp.einsum(
        "ihqk,ikhd->iqhd",
        probs.astype(jnp.bfloat16),
        triple[:, :, 2],
        preferred_element_type=jnp.float32,
    )
    attn_low = attended_rows.reshape(item_count * seq_len, hidden_width).astype(jnp.bfloat16)
    inner_output_rows = inner_rows_low(attn_low, a_in[:, 3 * rank_size : 4 * rank_size])
    first_sum = (
        hidden_rows
        + half_precision_product(attn_low, output_weight)
        + adapter_change(
            inner_output_rows, adapter_out_columns[:, 3 * hidden_width : 4 * hidden_width], 1
        )
    )
    middle = layer_norm(first_sum, gain_pair[0])
    middle_reduced = middle.astype(jnp.bfloat16)
    inner_up_rows = inner_rows_low(middle_reduced, a_in[:, 4 * rank_size : 5 * rank_size])
    upper_half = half_precision_product(middle_reduced, up_weight) + adapter_change(
        inner_up_rows, adapter_out_columns[:, 5 * hidden_width :], 1
    )
    active_low = jax.nn.gelu(upper_half).astype(jnp.bfloat16)
    inner_down_rows = inner_rows_low(active_low, a_down)
    second_sum = (
        middle
        + half_precision_product(active_low, down_weight)
        + adapter_change(
            inner_down_rows, adapter_out_columns[:, 4 * hidden_width : 5 * hidden_width], 1
        )
    )
    output = layer_norm(second_sum, gain_pair[1])
    saved = (
        qkv_low,
        log_total,
        attn_low,
        inner_attention_rows,
        inner_output_rows,
        first_sum,
        inner_up_rows,
        upper_half,
        inner_down_rows,
        second_sum,
    )
    return (output, saved)


def layer_backward(grad_output, saved, params, key_valid_mask, item_count, seq_len):
    (
        query_key_value_weight,
        output_weight,
        up_weight,
        down_weight,
        a_in,
        a_down,
        adapter_out_columns,
        gain_pair,
    ) = params
    (
        qkv_low,
        log_total,
        attn_low,
        inner_attention_rows,
        inner_output_rows,
        first_sum,
        inner_up_rows,
        upper_half,
        inner_down_rows,
        second_sum,
    ) = saved
    hidden_width = output_weight.shape[0]
    rank_size = a_down.shape[1]
    head_count = hidden_width // HDIM
    grad_second = norm_back(second_sum, gain_pair[1], grad_output)
    grad_lower = grad_second.astype(jnp.bfloat16)
    lower_half_input, down_adapter_gradient = adapter_backward(
        inner_down_rows,
        grad_lower,
        adapter_out_columns[:, 4 * hidden_width : 5 * hidden_width],
        a_down,
        1,
    )
    grad_active = dot_trans(grad_lower, down_weight) + lower_half_input
    unused_out, gelu_pull = jax.vjp(jax.nn.gelu, upper_half)
    grad_upper = gelu_pull(grad_active)[0].astype(jnp.bfloat16)
    upper_half_input, up_adapter_gradient = adapter_backward(
        inner_up_rows,
        grad_upper,
        adapter_out_columns[:, 5 * hidden_width :],
        a_in[:, 4 * rank_size : 5 * rank_size],
        1,
    )
    grad_middle = grad_second + dot_trans(grad_upper, up_weight) + upper_half_input
    grad_first = norm_back(first_sum, gain_pair[0], grad_middle)
    grad_branch = grad_first.astype(jnp.bfloat16)
    side_branch_input, output_adapter_gradient = adapter_backward(
        inner_output_rows,
        grad_branch,
        adapter_out_columns[:, 3 * hidden_width : 4 * hidden_width],
        a_in[:, 3 * rank_size : 4 * rank_size],
        1,
    )
    grad_attn = (dot_trans(grad_branch, output_weight) + side_branch_input).astype(jnp.bfloat16)
    triple, scores = attention_scores(qkv_low, key_valid_mask, item_count, seq_len, head_count)
    probs = jnp.exp(scores - log_total)
    grad_heads = grad_attn.reshape(item_count, seq_len, head_count, HDIM)
    grad_probs = jnp.einsum(
        "iqhd,ikhd->ihqk", grad_heads, triple[:, :, 2], preferred_element_type=jnp.float32
    )
    grad_value = jnp.einsum(
        "ihqk,iqhd->ikhd",
        probs.astype(jnp.bfloat16),
        grad_heads,
        preferred_element_type=jnp.float32,
    )
    row_dot = jnp.sum(grad_probs * probs, -1, keepdims=True)
    grad_scores = (probs * (grad_probs - row_dot)).astype(jnp.bfloat16)
    grad_query = jnp.einsum(
        "ihqk,ikhd->iqhd", grad_scores, triple[:, :, 1], preferred_element_type=jnp.float32
    ) * HDIM ** (-0.5)
    grad_key = jnp.einsum(
        "ihqk,iqhd->ikhd", grad_scores, triple[:, :, 0], preferred_element_type=jnp.float32
    ) * HDIM ** (-0.5)
    grad_qkv = jnp.stack([grad_query, grad_key, grad_value], 2).reshape(
        item_count * seq_len, 3 * hidden_width
    )
    grad_qkv = grad_qkv.astype(jnp.bfloat16)
    query_key_value_input, attention_adapter_gradient = adapter_backward(
        inner_attention_rows,
        grad_qkv,
        adapter_out_columns[:, : 3 * hidden_width],
        a_in[:, : 3 * rank_size],
        3,
    )
    grad_hidden = grad_first + dot_trans(grad_qkv, query_key_value_weight) + query_key_value_input
    adapter_out_gradient = jnp.concatenate(
        [
            attention_adapter_gradient,
            output_adapter_gradient,
            down_adapter_gradient,
            up_adapter_gradient,
        ],
        1,
    )
    return (grad_hidden, adapter_out_gradient)


def batch_grads(
    token_matrix,
    length_matrix,
    masked_selector,
    target_matrix,
    label_matrix,
    frozen_part,
    adapter_outputs,
    class_projection,
):
    (
        token_embedding_table,
        position_table,
        norm_gain_table,
        query_key_value_weight,
        output_weight,
        up_weight,
        down_weight,
        adapter_inputs,
        adapter_down_input,
        head_dense_maps,
    ) = frozen_part
    item_count, seq_len = token_matrix.shape
    vocab_rows, hidden_width = token_embedding_table.shape
    slot_count = masked_selector.shape[1]
    layer_count = query_key_value_weight.shape[0]
    vocab_start = lax.axis_index("vocab") * vocab_rows
    ids_all, targets_all, lengths_all = (
        lax.all_gather(token_matrix, "vocab", axis=0, tiled=True),
        lax.all_gather(target_matrix, "vocab", axis=0, tiled=True),
        lax.all_gather(length_matrix, "vocab", axis=0, tiled=True),
    )
    local_ids = ids_all - vocab_start
    inside = (local_ids >= 0) & (local_ids < vocab_rows)
    picked = jnp.take(token_embedding_table, jnp.clip(local_ids, 0, vocab_rows - 1), axis=0)
    terms = jnp.where(inside[..., None], picked.astype(jnp.float32), 0.0)
    looked = lax.psum_scatter(
        terms.astype(jnp.bfloat16), "vocab", scatter_dimension=0, tiled=True
    ).astype(jnp.float32)
    hidden_rows = layer_norm(
        looked + position_table.astype(jnp.float32), norm_gain_table[0]
    ).reshape(item_count * seq_len, hidden_width)
    key_valid_mask = jnp.arange(seq_len)[None, :] < length_matrix[:, None]
    layer_params = []
    saved_list = []
    for layer_number in range(layer_count):
        params = (
            query_key_value_weight[layer_number],
            output_weight[layer_number],
            up_weight[layer_number],
            down_weight[layer_number],
            adapter_inputs[layer_number],
            adapter_down_input[layer_number],
            adapter_outputs[layer_number],
            norm_gain_table[1 + 2 * layer_number : 3 + 2 * layer_number],
        )
        hidden_rows, saved = layer_forward(hidden_rows, params, key_valid_mask, item_count, seq_len)
        layer_params.append(params)
        saved_list.append(saved)
    final_low = hidden_rows.reshape(item_count, seq_len, hidden_width).astype(jnp.bfloat16)
    slot_hot = (masked_selector[..., None] == jnp.arange(seq_len)).astype(jnp.bfloat16)
    picked_rows = (
        jnp.einsum("isl,ild->isd", slot_hot, final_low, preferred_element_type=jnp.float32)
        .astype(jnp.bfloat16)
        .reshape(item_count * slot_count, hidden_width)
    )
    pre_mask = half_precision_product(picked_rows, head_dense_maps[0])
    mask_gain = norm_gain_table[2 * layer_count + 1]
    feature_low = layer_norm(jax.nn.gelu(pre_mask), mask_gain).astype(jnp.bfloat16)
    features_all = lax.all_gather(feature_low, "vocab", axis=0, tiled=True)
    logits = dot_trans(features_all, token_embedding_table)
    target_flat = targets_all.reshape(-1)
    target_hot = jnp.arange(vocab_rows)[None, :] + vocab_start == target_flat[:, None]
    target_local = jnp.sum(jnp.where(target_hot, logits, 0.0), -1)
    local_top = jnp.max(logits, -1)
    row_top = lax.pmax(local_top, "vocab")
    row_total, row_target = lax.psum(
        (jnp.sum(jnp.exp(logits - row_top[:, None]), -1), target_local), "vocab"
    )
    log_total = row_top + jnp.log(row_total)
    live_all = (jnp.arange(slot_count)[None, :] < lengths_all[:, None] * 15 // 100).reshape(-1)
    grad_logits = (
        (jnp.exp(logits - log_total[:, None]) - target_hot.astype(jnp.float32))
        * live_all[:, None].astype(jnp.float32)
    ).astype(jnp.bfloat16)
    grad_feature = lax.psum_scatter(
        half_precision_product(grad_logits, token_embedding_table).astype(jnp.bfloat16),
        "vocab",
        scatter_dimension=0,
        tiled=True,
    ).astype(jnp.float32)
    own_start = lax.axis_index("vocab") * item_count * slot_count
    own_loss = lax.dynamic_slice_in_dim(
        log_total - row_target, own_start, item_count * slot_count, 0
    )
    own_live = lax.dynamic_slice_in_dim(live_all, own_start, item_count * slot_count, 0)
    unused_out, head_pull = jax.vjp(
        lambda values: layer_norm(jax.nn.gelu(values), mask_gain), pre_mask
    )
    grad_pre = head_pull(grad_feature)[0].astype(jnp.bfloat16)
    grad_rows = dot_trans(grad_pre, head_dense_maps[0]).reshape(
        item_count, slot_count, hidden_width
    )
    item_index = jnp.broadcast_to(jnp.arange(item_count)[:, None], masked_selector.shape)
    grad_final = (
        jnp.zeros((item_count, seq_len, hidden_width), jnp.float32)
        .at[item_index, masked_selector]
        .add(grad_rows)
    )
    pooled = jnp.tanh(half_precision_product(final_low[:, 0, :], head_dense_maps[1]))
    class_logits = precise_product(pooled, class_projection[:-1]) + class_projection[-1:]
    class_top = jnp.max(class_logits, -1, keepdims=True)
    class_exp = jnp.exp(class_logits - class_top)
    class_sum = jnp.sum(class_exp, -1, keepdims=True)
    label_hot = (jnp.arange(class_logits.shape[1])[None, :] == label_matrix[:, None]).astype(
        jnp.float32
    )
    class_loss = jnp.sum(
        class_top[:, 0] + jnp.log(class_sum[:, 0]) - jnp.sum(class_logits * label_hot, -1)
    )
    grad_class = class_exp / class_sum - label_hot
    grad_head = jnp.concatenate(
        [precise_product(pooled.T, grad_class), jnp.sum(grad_class, 0, keepdims=True)], 0
    )
    grad_pooled = precise_product(grad_class, class_projection[:-1].T)
    grad_pre_class = (grad_pooled * (1.0 - pooled * pooled)).astype(jnp.bfloat16)
    grad_final = grad_final.at[:, 0, :].add(dot_trans(grad_pre_class, head_dense_maps[1]))
    grad_hidden = grad_final.reshape(item_count * seq_len, hidden_width)
    grad_list = [None] * layer_count
    for layer_number in reversed(range(layer_count)):
        grad_hidden, grad_list[layer_number] = layer_backward(
            grad_hidden,
            saved_list[layer_number],
            layer_params[layer_number],
            key_valid_mask,
            item_count,
            seq_len,
        )
    loss_local = jnp.sum(jnp.where(own_live, own_loss, 0.0)) + class_loss
    count_local = (jnp.sum(own_live.astype(jnp.int32)) + item_count).astype(jnp.float32)
    return (jnp.stack(grad_list), grad_head, jnp.stack([loss_local, count_local]))


def moment_update(weight, grad, first, second):
    first_new = BETA_ONE * first + (1.0 - BETA_ONE) * grad
    second_new = BETA_TWO * second + (1.0 - BETA_TWO) * grad * grad
    fix_one = 1.0 - BETA_ONE**STEP
    fix_two = 1.0 - BETA_TWO**STEP
    step_size = first_new / fix_one / (jnp.sqrt(second_new / fix_two) + ADAM_EPS)
    return (weight - RATE * (step_size + DECAY * weight), first_new, second_new)


def body(
    input_token_ids,
    lengths,
    masked_positions,
    masked_token_targets,
    labels,
    token_embedding_table,
    position_table,
    norm_gain_table,
    query_key_value_weight,
    output_weight,
    up_weight,
    down_weight,
    adapter_inputs,
    adapter_down_input,
    head_dense_maps,
    adapter_outputs,
    class_projection,
    adapter_moment_first,
    adapter_moment_second,
    class_moment_first,
    class_moment_second,
):
    frozen_part = (
        token_embedding_table,
        position_table,
        norm_gain_table,
        query_key_value_weight,
        output_weight,
        up_weight,
        down_weight,
        adapter_inputs,
        adapter_down_input,
        head_dense_maps,
    )
    adapter_out_sum = jnp.zeros(adapter_outputs.shape, jnp.float32)
    sum_head = jnp.zeros(class_projection.shape, jnp.float32)
    sum_stats = jnp.zeros((2,), jnp.float32)
    for batch_index in range(input_token_ids.shape[0]):
        adapter_out_gradient, grad_head, stats = batch_grads(
            input_token_ids[batch_index],
            lengths[batch_index],
            masked_positions[batch_index],
            masked_token_targets[batch_index],
            labels[batch_index],
            frozen_part,
            adapter_outputs,
            class_projection,
        )
        adapter_out_gradient, grad_head, stats = lax.psum(
            (adapter_out_gradient, grad_head, stats), ("dp", "vocab")
        )
        adapter_out_sum = adapter_out_sum + adapter_out_gradient
        sum_head = sum_head + grad_head
        sum_stats = sum_stats + stats
    adapter_out_gradient = adapter_out_sum / sum_stats[1]
    grad_head = sum_head / sum_stats[1]
    overall_norm = jnp.sqrt(
        jnp.sum(adapter_out_gradient * adapter_out_gradient) + jnp.sum(grad_head * grad_head)
    )
    multiplier = CLIP_AT / jnp.maximum(overall_norm, CLIP_AT)
    adapter_outputs_next, adapter_moment_first_next, adapter_moment_second_next = moment_update(
        adapter_outputs,
        adapter_out_gradient * multiplier,
        adapter_moment_first,
        adapter_moment_second,
    )
    class_projection_next, class_moment_first_next, class_moment_second_next = moment_update(
        class_projection, grad_head * multiplier, class_moment_first, class_moment_second
    )
    return (
        sum_stats,
        overall_norm.reshape(1),
        adapter_outputs_next,
        adapter_moment_first_next,
        adapter_moment_second_next,
        class_projection_next,
        class_moment_first_next,
        class_moment_second_next,
    )


def solution(mesh):
    placed = (
        P(None, ("dp", "vocab"), None),
        P(None, ("dp", "vocab")),
        P(None, ("dp", "vocab"), None),
        P(None, ("dp", "vocab"), None),
        P(None, ("dp", "vocab")),
        P("vocab", None),
        P(),
        P(),
        P(),
        P(),
        P(),
        P(),
        P(),
        P(),
        P(),
        P(),
        P(),
        P(),
        P(),
        P(),
        P(),
    )
    return jax.shard_map(
        body,
        mesh=mesh,
        in_specs=placed,
        out_specs=(P(), P(), P(), P(), P(), P(), P(), P()),
        check_vma=False,
    )
```

profile of v0, /device:TPU:0, one launch (start us, length us, event | category | flops | bytes accessed | tf_op | source)
XLA Modules:
  0.0 953.4 jit_solution(7300684170570763515)
XLA Ops:
  14.2 17.4 %gather_fusion.1 = bf16[2048,768]{1,0:T(8,128)(2,1)S(1)} fusion(bf16[12576,768]{1,0:T(8,128)(2,1)} %param.32, s32[2048]{0:T(1024)S(1)} %broadcast_clamp_fusion), kind=kCustom, calls=%fused_computation.1.clone | custom fusion | bytes 6299648 | tf_op jit(solution)/shard_map/jit(_take)/gather | solution.py:301
  39.4 19.0 %gather_fusion = bf16[2048,768]{1,0:T(8,128)(2,1)S(1)} fusion(bf16[12576,768]{1,0:T(8,128)(2,1)} %param.32, s32[2048]{0:T(1024)S(1)} %broadcast_clamp_fusion.1), kind=kCustom, calls=%fused_computation.clone | custom fusion | bytes 6299648 | tf_op jit(solution)/shard_map/jit(_take)/gather | solution.py:301
  95.1 19.4 %reduce-scatter.7.cloned.1.call-done = bf16[1,512,768]{2,1,0:T(8,128)(2,1)} async-done(((bf16[4,512,768]{2,1,0:T(8,128)(2,1)}), bf16[1,512,768]{2,1,0:T(8,128)(2,1)}) %reduce-scatter.7.cloned.1.call-update) | async-done | bytes 786448 | tf_op jit(solution)/shard_map/reduce_scatter | solution.py:303
  207.4 9.0 multiply_convert_fusion.5
  252.4 7.1 fusion.107
  295.1 7.1 fusion.109
  329.2 7.2 multiply_convert_fusion.4
  397.0 8.6 all-gather.7
  412.7 14.2 %fusion.505 = (f32[304]{0:T(512)}, f32[304,12576]{1,0:T(8,128)}) fusion(bf16[304,768]{1,0:T(8,128)(2,1)} %reshape.1845, bf16[12576,768]{1,0:T(8,128)(2,1)} %param.32), kind=kOutput, calls=%fused_computation.798 | convolution fusion | flops 5876110336 | bytes 35077312 | tf_op jit(solution)/shard_map/dot_general | solution.py:33
  427.0 14.2 %fusion.504 = (f32[304]{0:T(512)}, f32[304,12576]{1,0:T(8,128)}) fusion(bf16[304,768]{1,0:T(8,128)(2,1)} %reshape.1843, bf16[12576,768]{1,0:T(8,128)(2,1)} %param.32), kind=kOutput, calls=%fused_computation.797 | convolution fusion | flops 5876110336 | bytes 35077312 | tf_op jit(solution)/shard_map/dot_general | solution.py:33
  441.2 7.4 all-reduce.11
  448.6 13.8 %fusion.6 = (f32[304]{0:T(512)}, f32[304]{0:T(512)}, f32[304]{0:T(512)}, f32[304]{0:T(512)}) fusion(f32[304,12576]{1,0:T(8,128)} %get-tuple-element.168, s32[12576]{0:T(1024)} %iota_add_fusion, s32[304]{0:T(512)} %eq.131, f32[304]{0:T(512)} %get-tuple-element.68, f32[304,12576]{1,0:T(8,128)} %get-tuple-element.166, f32[304]{0:T(512)} %get-tuple-element.67, ...), kind=kLoop, calls=%fused_computation.12 | loop fusion | flops 38229824 | bytes 30644864 | tf_op jit(solution)/shard_map/reduce_sum | solution.py:340
  470.6 17.8 %fusion.184 = bf16[304,768]{1,0:T(8,128)(2,1)} fusion(bf16[12576,768]{1,0:T(8,128)(2,1)} %param.32, f32[304,12576]{1,0:T(8,128)} %get-tuple-element.166, f32[304]{0:T(512)} %convert_element_type.611, f32[304]{0:T(512)S(1)} %get-tuple-element.98, s32[12576]{0:T(1024)} %iota_add_fusion, s32[304]{0:T(512)} %eq.121), kind=kOutput, calls=%fused_computation.310 | convolution fusion | flops 5895459840 | bytes 35130048 | tf_op jit(solution)/shard_map/dot_general | solution.py:29
  489.1 18.2 %fusion.187 = bf16[304,768]{1,0:T(8,128)(2,1)} fusion(bf16[12576,768]{1,0:T(8,128)(2,1)} %param.32, f32[304,12576]{1,0:T(8,128)} %get-tuple-element.168, f32[304]{0:T(512)S(1)} %copy-done.199, f32[304]{0:T(512)S(1)} %get-tuple-element.96, s32[12576]{0:T(1024)S(1)} %copy-done.81, s32[304]{0:T(512)S(1)} %copy-done.195), kind=kOutput, calls=%fused_computation.311 | convolution fusion | flops 5895459840 | bytes 35130048 | tf_op jit(solution)/shard_map/dot_general | solution.py:29
  507.3 13.9 %fusion.474 = (bf16[80,768]{1,0:T(8,128)(2,1)}, bf16[80,768]{1,0:T(8,128)(2,1)}) fusion(bf16[304,768]{1,0:T(8,128)(2,1)} %fusion.187, bf16[304,768]{1,0:T(8,128)(2,1)} %fusion.184), kind=kCustom, calls=%all-reduce-scatter.2 | all-reduce-scatter fusion | flops 491521 | bytes 1180160
  601.9 7.1 fusion.43
  627.0 8.9 multiply_reduce_fusion.3
  684.9 7.7 fusion.162
  692.6 8.9 multiply_reduce_fusion.2
  720.2 8.9 multiply_reduce_fusion.1
  780.3 8.9 multiply_reduce_fusion
  789.2 7.1 multiply_convert_fusion
  811.6 39.7 %all-reduce.9 = (f32[2]{0:T(128)S(1)}, f32[769,3]{0,1:T(4,128)S(1)}) all-reduce(f32[2]{0:T(128)S(1)} %maximum_add_fusion.2, f32[769,3]{0,1:T(4,128)S(1)} %copy-done.132), channel_id=1, replica_groups=mesh['dp'=8,'vocab'=4] {'dp','vocab'}, use_global_device_ids=true, to_apply=%region_28.30 | all-reduce | flops 2309 | bytes 18472 | tf_op jit(solution)/shard_map/psum | solution.py:468
  853.1 84.5 %all-reduce.15.cloned.1.call-done = f32[2,8,6912]{2,1,0:T(8,128)} async-done(((f32[2,8,6912]{2,1,0:T(8,128)}), f32[2,8,6912]{2,1,0:T(8,128)}) %all-reduce.15.cloned.1.call-update) | async-done | bytes 442384 | tf_op jit(solution)/shard_map/psum | solution.py:468
  (931 shorter events, 549.7 us)
Async XLA Ops:
  7.2 87.9 %reduce-scatter.9.cloned.1.call-start = ((), (), s32[]{:S(2)}) async-start(), calls=%async_computation.3 | async-start | bytes 3932160 | tf_op jit(solution)/shard_map/reduce_scatter | solution.py:303
  33.8 80.6 %reduce-scatter.7.cloned.1.call-start = ((), (), s32[]{:S(2)}) async-start(), calls=%async_computation.2 | async-start | bytes 3932160 | tf_op jit(solution)/shard_map/reduce_scatter | solution.py:303
  60.7 53.8 %copy-start.26 = (bf16[512,768]{1,0:T(8,128)(2,1)S(1)}, bf16[512,768]{1,0:T(8,128)(2,1)}, u32[]{:S(2)}) copy-start(bf16[512,768]{1,0:T(8,128)(2,1)} %param.33) | copy-start | bytes 2359300
  60.7 876.9 %all-reduce.15.cloned.1.call-start = ((), (), s32[]{:S(2)}) async-start(), calls=%async_computation.4 | async-start | bytes 884736 | tf_op jit(solution)/shard_map/psum | solution.py:468
  88.8 143.0 %copy-start.40 = (f32[8,6912]{1,0:T(8,128)}, f32[8,6912]{1,0:T(8,128)S(1)}, u32[]{:S(2)}) copy-start(f32[8,6912]{1,0:T(8,128)S(1)} %get-tuple-element.100) | copy-start | bytes 663556
  89.4 189.4 %copy-start.61 = (f32[8,2304]{1,0:T(8,128)}, f32[8,2304]{1,0:T(8,128)S(1)}, u32[]{:S(2)}) copy-start(f32[8,2304]{1,0:T(8,128)S(1)} %slice.422) | copy-start | bytes 221188
  92.8 139.0 %copy-start.82 = (f32[768]{0:T(1024)}, f32[768]{0:T(1024)S(1)}, u32[]{:S(2)}) copy-start(f32[768]{0:T(1024)S(1)} %get-tuple-element.46) | copy-start | bytes 9220
  92.8 229.2 %copy-start.84 = (f32[768]{0:T(1024)}, f32[768]{0:T(1024)S(1)}, u32[]{:S(2)}) copy-start(f32[768]{0:T(1024)S(1)} %get-tuple-element.45) | copy-start | bytes 9220
  231.4 90.6 %copy-start.6 = (f32[512,768]{1,0:T(8,128)}, f32[512,768]{1,0:T(8,128)S(1)}, u32[]{:S(2)}) copy-start(f32[512,768]{1,0:T(8,128)S(1)} %get-tuple-element.144) | copy-start | bytes 4718596
  231.5 90.6 %copy-start.109 = (f32[512]{0:T(512)}, f32[512]{0:T(512)S(1)}, u32[]{:S(2)}) copy-start(f32[512]{0:T(512)S(1)} %broadcast_multiply_fusion.4) | copy-start | bytes 6148
  231.8 90.2 %copy-start.151 = (f32[512]{0:T(512)}, f32[512]{0:T(512)S(1)}, u32[]{:S(2)}) copy-start(f32[512]{0:T(512)S(1)} %fusion.437) | copy-start | bytes 6148
  233.1 87.0 %copy-start.10 = (f32[512,768]{1,0:T(8,128)}, f32[512,768]{1,0:T(8,128)S(1)}, u32[]{:S(2)}) copy-start(f32[512,768]{1,0:T(8,128)S(1)} %get-tuple-element.140) | copy-start | bytes 4718596
  233.1 87.0 %copy-start.113 = (f32[512]{0:T(512)}, f32[512]{0:T(512)S(1)}, u32[]{:S(2)}) copy-start(f32[512]{0:T(512)S(1)} %broadcast_multiply_fusion.9) | copy-start | bytes 6148
  233.4 86.7 %copy-start.155 = (f32[512]{0:T(512)}, f32[512]{0:T(512)S(1)}, u32[]{:S(2)}) copy-start(f32[512]{0:T(512)S(1)} %fusion.433) | copy-start | bytes 6148
  276.5 43.6 %copy-start.123 = (bf16[512,8]{0,1:T(8,128)(2,1)}, bf16[512,8]{0,1:T(8,128)(2,1)S(1)}, u32[]{:S(2)}) copy-start(bf16[512,8]{0,1:T(8,128)(2,1)S(1)} %convolution_convert_fusion.14) | copy-start | bytes 24580
  523.9 17.1 %collective-permute-start = (bf16[12,768]{1,0:T(8,128)(2,1)}, bf16[12,768]{1,0:T(8,128)(2,1)}, u32[]{:S(2)}, u32[]{:S(2)}) collective-permute-start(bf16[12,768]{1,0:T(8,128)(2,1)} %slice.441), channel_id=1, source_target_pairs={{0,1},{1,2},{2,3},{4,5},{5,6},{6,7},{8,9},{9,10},{10,11},{12,13},{... | collective-permute-start | bytes 55304
  525.8 18.2 %collective-permute-start.1 = (bf16[12,768]{1,0:T(8,128)(2,1)}, bf16[12,768]{1,0:T(8,128)(2,1)}, u32[]{:S(2)}, u32[]{:S(2)}) collective-permute-start(bf16[12,768]{1,0:T(8,128)(2,1)} %slice.442), channel_id=1, source_target_pairs={{0,1},{1,2},{2,3},{4,5},{5,6},{6,7},{8,9},{9,10},{10,11},{12,13},{... | collective-permute-start | bytes 55304
  810.0 131.2 %copy-start.89 = (f32[769,3]{0,1:T(4,128)S(1)}, f32[769,3]{0,1:T(4,128)}, u32[]{:S(2)}) copy-start(f32[769,3]{0,1:T(4,128)} %param.43) | copy-start | bytes 27688
  810.0 131.2 %copy-start.187 = (f32[769,3]{0,1:T(4,128)S(1)}, f32[769,3]{0,1:T(4,128)}, u32[]{:S(2)}) copy-start(f32[769,3]{0,1:T(4,128)} %param.46) | copy-start | bytes 27688
  810.0 131.2 %copy-start.188 = (f32[769,3]{0,1:T(4,128)S(1)}, f32[769,3]{0,1:T(4,128)}, u32[]{:S(2)}) copy-start(f32[769,3]{0,1:T(4,128)} %param.47) | copy-start | bytes 27688
  810.1 132.4 %copy-start.46 = (f32[2,8,6912]{2,1,0:T(8,128)S(1)}, f32[2,8,6912]{2,1,0:T(8,128)}, u32[]{:S(2)}) copy-start(f32[2,8,6912]{2,1,0:T(8,128)} %param.42) | copy-start | bytes 1327108
  810.1 132.4 %copy-start.72 = (f32[2,8,6912]{2,1,0:T(8,128)S(1)}, f32[2,8,6912]{2,1,0:T(8,128)}, u32[]{:S(2)}) copy-start(f32[2,8,6912]{2,1,0:T(8,128)} %param.44) | copy-start | bytes 1327108
  810.1 132.4 %copy-start.73 = (f32[2,8,6912]{2,1,0:T(8,128)S(1)}, f32[2,8,6912]{2,1,0:T(8,128)}, u32[]{:S(2)}) copy-start(f32[2,8,6912]{2,1,0:T(8,128)} %param.45) | copy-start | bytes 1327108
  851.3 94.0 %copy-start.219 = (f32[2]{0:T(128)}, f32[2]{0:T(128)S(1)}, u32[]{:S(2)}) copy-start(f32[2]{0:T(128)S(1)} %get-tuple-element.61) | copy-start | bytes 28
  (254 other events, 1836.6 us)
Sparse Core Ops, SparseCore 0:
  33.9 39.7 reduce-scatter.8
  76.4 37.9 reduce-scatter.6
  811.6 125.8 all-reduce.14
where the time goes:
time: 964 us; the launch traced here: 953 us
  matrix products  409 us (42%)
  local copies, waits for them, and re-layouts  168 us (17%)
  other arithmetic  129 us (13%)
  blocking collectives  111 us (12%)
  waiting for transfers between devices  104 us (11%)
  between operations  27.6 us (3%)
    dot_general x38, matrix products, half_precision_product(): return jnp.dot(left, right, preferred_element_type=jnp.float32)  108 us
    dot_general x34, matrix products, dot_trans(): lax.dot_general(left, right, (((1,), (1,)), ((), ())), preferred_element_...  99.7 us
    psum x1, waiting for transfers between devices, body(): lax.psum((adapter_out_gradient, grad_head, stats), ('dp', 'vocab'))  84.5 us
    dot_general x16, matrix products, adapter_change(): jnp.einsum('bhx,xhs->bhs', block_list, adapter_out_blocks, precision=FULL...  56.3 us
    mul x8, local copies, waits for them, and re-layouts, adapter_change(): ADAPTER_SCALE * jnp.einsum('bhx,xhs->bhs', block_list, adapter_out_blocks...  49.2 us
    psum x1, blocking collectives, body(): lax.psum((adapter_out_gradient, grad_head, stats), ('dp', 'vocab'))  39.7 us
    unnamed x560, local copies, waits for them, and re-layouts  38.5 us
    gather x2, local copies, waits for them, and re-layouts, batch_grads(): jnp.take(token_embedding_table, jnp.clip(local_ids, 0, vocab_rows - 1), a...  36.5 us
  transfers between devices with their start and end apart: 5, of which 2 were waited for; matrix products, arithmetic and copies ran while one was open for 5% of the time, Pallas kernels for 0%

commit v1 on v0

v1 whole, which is shorter than its diff:
```python
import jax
import jax.numpy as jnp
from jax import lax
from jax.sharding import PartitionSpec as P

HDIM = 64
STEP = 10
NORM_EPS = 1e-05
ADAPTER_SCALE = 2.0
NEG_FILL = -1e30
CLIP_AT = 0.001
RATE = 0.03
BETA_ONE = 0.9
BETA_TWO = 0.999
ADAM_EPS = 1e-08
DECAY = 0.01
BF = jnp.bfloat16
F32 = jnp.float32


def dot(left, right):
    return jnp.dot(left, right, preferred_element_type=F32)


def dot_nt(left, right):
    return lax.dot_general(left, right, (((1,), (1,)), ((), ())), preferred_element_type=F32)


def dot_tn(left, right):
    return lax.dot_general(left, right, (((0,), (0,)), ((), ())), preferred_element_type=F32)


def norm_parts(values):
    center = values - jnp.mean(values, -1, keepdims=True)
    spread = jnp.mean(center * center, -1, keepdims=True)
    rstd = lax.rsqrt(spread + NORM_EPS)
    return center * rstd, rstd


def norm_back(grad_hat, hat, rstd):
    first = jnp.mean(grad_hat, -1, keepdims=True)
    second = jnp.mean(grad_hat * hat, -1, keepdims=True)
    return rstd * (grad_hat - first - hat * second)


def gelu_both(values):
    root = 0.7978845608028654
    square = values * values
    bend = jnp.tanh(root * values * (1.0 + 0.044715 * square))
    half = 0.5 * (1.0 + bend)
    slope = half + 0.5 * values * (1.0 - bend * bend) * root * (1.0 + 0.134145 * square)
    return values * half, slope


def high_low(values):
    high = lax.reduce_precision(values, 8, 7)
    return high.astype(BF), (values - high).astype(BF)


def swap(value, axis, mask):
    size = lax.axis_size(axis)
    return lax.ppermute(value, axis, [(i, i ^ mask) for i in range(size)])


def deliver(parts):
    size = parts.shape[0]
    if size & (size - 1):
        return lax.psum_scatter(parts, "vocab", scatter_dimension=0, tiled=True)[0]
    index = lax.axis_index("vocab")
    core = index % 2
    pairs = parts.reshape((size // 2, 2) + parts.shape[1:])
    mine = lax.dynamic_index_in_dim(pairs, core, 1, keepdims=False)
    other = lax.dynamic_index_in_dim(pairs, 1 - core, 1, keepdims=False)
    mine = mine + swap(other, "vocab", 1)
    row = index // 2
    total = lax.dynamic_index_in_dim(mine, row, 0, keepdims=False)
    for mask in range(1, size // 2):
        sent = lax.dynamic_index_in_dim(mine, row ^ mask, 0, keepdims=False)
        total = total + swap(sent, "vocab", 2 * mask)
    return total


def reduce_all(flat):
    rows = flat.shape[0]
    steps = []
    for axis in ("vocab", "dp"):
        size = lax.axis_size(axis)
        mask = 1
        while mask < size:
            steps.append((axis, mask))
            mask *= 2
    pad = -rows % (8 << len(steps))
    now = jnp.pad(flat, ((0, pad), (0, 0)))
    for axis, mask in steps:
        bit = (lax.axis_index(axis) // mask) % 2
        half = now.shape[0] // 2
        keep = lax.dynamic_slice_in_dim(now, bit * half, half)
        send = lax.dynamic_slice_in_dim(now, (1 - bit) * half, half)
        now = keep + swap(send, axis, mask)
    for axis, mask in reversed(steps):
        bit = (lax.axis_index(axis) // mask) % 2
        got = swap(now, axis, mask)
        now = jnp.where(bit == 0, jnp.concatenate([now, got]), jnp.concatenate([got, now]))
    return now[:rows]


def adapter_tables(adapter_inputs, adapter_down_input, adapter_outputs):
    layers, width, columns = adapter_inputs.shape
    rank = adapter_down_input.shape[2]
    total = adapter_outputs.shape[2]
    one = jnp.pad(adapter_inputs, ((0, 0), (0, 0), (0, 64 - columns)))
    a_all = jnp.concatenate([one, one], 2)
    one = jnp.pad(adapter_down_input, ((0, 0), (0, 0), (columns, 64 - columns - rank)))
    a_down = jnp.concatenate([one, one], 2)
    high = lax.reduce_precision(ADAPTER_SCALE * adapter_outputs, 8, 7)
    both = jnp.stack([high, ADAPTER_SCALE * adapter_outputs - high], 1)
    column = jnp.arange(total) // width
    group = jnp.where(column < 4, column, jnp.where(column == 4, 5, 4))
    keep = jnp.arange(8)[:, None] == group[None, :]
    b_all = jnp.where(keep[None, None, :, None, :], both[:, :, None, :, :], 0.0)
    return a_all, a_down, b_all.reshape(layers, 128, total).astype(BF)


def heads(rows):
    return rows.reshape(rows.shape[0], -1, HDIM)


def attend(q, k, v, length):
    scores = jnp.einsum("qhd,khd->hqk", heads(q), heads(k), preferred_element_type=F32)
    valid = jnp.arange(k.shape[0]) < length
    scores = jnp.where(valid, scores * HDIM**-0.5, NEG_FILL)
    top = jnp.max(scores, -1, keepdims=True)
    exponent = jnp.exp(scores - top)
    total = jnp.sum(exponent, -1, keepdims=True)
    out = jnp.einsum("hqk,khd->qhd", (exponent / total).astype(BF), heads(v), preferred_element_type=F32)
    return out.reshape(q.shape).astype(BF), top + jnp.log(total)


def attend_back(q, k, v, length, log_total, grad):
    scores = jnp.einsum("qhd,khd->hqk", heads(q), heads(k), preferred_element_type=F32)
    valid = jnp.arange(k.shape[0]) < length
    scores = jnp.where(valid, scores * HDIM**-0.5, NEG_FILL)
    probs = jnp.exp(scores - log_total)
    grad_probs = jnp.einsum("qhd,khd->hqk", heads(grad), heads(v), preferred_element_type=F32)
    grad_v = jnp.einsum("hqk,qhd->khd", probs.astype(BF), heads(grad), preferred_element_type=F32)
    row = jnp.sum(grad_probs * probs, -1, keepdims=True)
    grad_scores = (probs * (grad_probs - row)).astype(BF)
    grad_q = jnp.einsum("hqk,khd->qhd", grad_scores, heads(k), preferred_element_type=F32) * HDIM**-0.5
    grad_k = jnp.einsum("hqk,qhd->khd", grad_scores, heads(q), preferred_element_type=F32) * HDIM**-0.5
    return (
        grad_q.reshape(q.shape).astype(BF),
        grad_k.reshape(k.shape).astype(BF),
        grad_v.reshape(k.shape).astype(BF),
    )


def upper_part(hidden, attn, weights, gains):
    (_, wo, wu, wd, a_all, a_down, b_all) = weights
    width = wo.shape[0]
    inner_o = dot(attn, a_all).astype(BF)
    first = hidden + dot(attn, wo) + dot(inner_o, b_all[:, 3 * width : 4 * width])
    hat1, rstd1 = norm_parts(first)
    mid = hat1 * gains[0]
    low = mid.astype(BF)
    inner_u = dot(low, a_all).astype(BF)
    upper = dot(low, wu) + dot(inner_u, b_all[:, 5 * width :])
    active, slope = gelu_both(upper)
    active = active.astype(BF)
    inner_d = dot(active, a_down).astype(BF)
    second = mid + dot(active, wd) + dot(inner_d, b_all[:, 4 * width : 5 * width])
    hat2, rstd2 = norm_parts(second)
    lane = jnp.arange(128) % 64 // 8
    inner = jnp.where(lane == 3, inner_o, jnp.where(lane == 4, inner_u, inner_d))
    return hat2 * gains[1], (hat1.astype(BF), rstd1, slope.astype(BF), hat2.astype(BF), rstd2, inner)


def upper_back(grad, saved, weights, gains):
    (_, wo, wu, wd, a_all, a_down, b_all) = weights
    width = wo.shape[0]
    hat1, rstd1, slope, hat2, rstd2, inner = saved
    grad2 = norm_back(grad * gains[1], hat2.astype(F32), rstd2)
    low = grad2.astype(BF)
    d_inner = dot_nt(low, b_all[:, 4 * width : 5 * width]).astype(BF)
    grad_active = dot_nt(low, wd) + dot_nt(d_inner, a_down)
    b_down = dot_tn(inner, low)[40:48]
    grad_upper = (grad_active * slope.astype(F32)).astype(BF)
    d_inner = dot_nt(grad_upper, b_all[:, 5 * width :]).astype(BF)
    grad_mid = grad2 + dot_nt(grad_upper, wu) + dot_nt(d_inner, a_all)
    b_up = dot_tn(inner, grad_upper)[32:40]
    grad1 = norm_back(grad_mid * gains[0], hat1.astype(F32), rstd1)
    low = grad1.astype(BF)
    d_inner = dot_nt(low, b_all[:, 3 * width : 4 * width]).astype(BF)
    grad_attn = (dot_nt(low, wo) + dot_nt(d_inner, a_all)).astype(BF)
    b_out = dot_tn(inner, low)[24:32]
    return grad1, grad_attn, ADAPTER_SCALE * jnp.concatenate([b_out, b_down, b_up], 1)


def first_layer(length, rows, positions, gain, gains, weights):
    wqkv, a_all, b_all = weights[0], weights[4], weights[6]
    width = rows.shape[1]
    hat0, _ = norm_parts(rows.astype(F32) + positions.astype(F32))
    hidden = hat0 * gain
    low = hidden.astype(BF)
    inner = dot(low, a_all).astype(BF)
    qkv = (dot(low, wqkv) + dot(inner, b_all[:, : 3 * width])).astype(BF)
    q, k, v = (qkv[:, i * width : (i + 1) * width] for i in range(3))
    attn, log_total = attend(q, k, v, length)
    out, saved = upper_part(hidden, attn, weights, gains)
    return high_low(out), (q, k, v, log_total, inner) + saved


def first_back(length, grad, saved, weights, gains):
    q, k, v, log_total, inner = saved[:5]
    _, grad_attn, b_rest = upper_back(grad, saved[5:], weights, gains)
    grads = attend_back(q, k, v, length, log_total, grad_attn)
    b_qkv = [dot_tn(inner, g)[8 * i : 8 * i + 8] for i, g in enumerate(grads)]
    return jnp.concatenate([ADAPTER_SCALE * jnp.concatenate(b_qkv, 1), b_rest], 1)


def last_layer(length, high, low, picks, gains, weights):
    wqkv, a_all, b_all = weights[0], weights[4], weights[6]
    width = high.shape[1]
    hot = (picks[:, None] == jnp.arange(high.shape[0])[None, :]).astype(BF)
    x = dot(hot, high).astype(BF)
    hidden = x.astype(F32) + dot(hot, low)
    inner_q = dot(x, a_all).astype(BF)
    q = (dot(x, wqkv[:, :width]) + dot(inner_q, b_all[:, :width])).astype(BF)
    inner = dot(high, a_all).astype(BF)
    kv = (dot(high, wqkv[:, width:]) + dot(inner, b_all[:, width : 3 * width])).astype(BF)
    k, v = kv[:, :width], kv[:, width:]
    attn, log_total = attend(q, k, v, length)
    out, saved = upper_part(hidden, attn, weights, gains)
    return out.astype(BF), (hot, q, k, v, log_total, inner_q, inner) + saved


def last_back(length, grad, saved, weights, gains):
    wqkv, a_all, b_all = weights[0], weights[4], weights[6]
    hot, q, k, v, log_total, inner_q, inner = saved[:7]
    width = q.shape[1]
    grad1, grad_attn, b_rest = upper_back(grad, saved[7:], weights, gains)
    d_q, d_k, d_v = attend_back(q, k, v, length, log_total, grad_attn)
    d_inner = dot_nt(d_q, b_all[:, :width]).astype(BF)
    picked = grad1 + dot_nt(d_q, wqkv[:, :width]) + dot_nt(d_inner, a_all)
    high, low = high_low(picked)
    d_kv = jnp.concatenate([d_k, d_v], 1)
    d_inner = dot_nt(d_kv, b_all[:, width : 3 * width]).astype(BF)
    out = dot_nt(d_kv, wqkv[:, width:]) + dot_nt(d_inner, a_all) + dot_tn(hot, high) + dot_tn(hot, low)
    b_qkv = [dot_tn(inner_q, d_q)[0:8], dot_tn(inner, d_k)[8:16], dot_tn(inner, d_v)[16:24]]
    return out, jnp.concatenate([ADAPTER_SCALE * jnp.concatenate(b_qkv, 1), b_rest], 1)


def table_pass(features, table):
    logits = dot_nt(features, table)
    top = jnp.max(logits, -1, keepdims=True)
    exponent = jnp.exp(logits - top)
    total = jnp.sum(exponent, -1, keepdims=True)
    return dot(exponent.astype(BF), table) / total, top, total


def moment_update(weight, grad, first, second):
    first_new = BETA_ONE * first + (1.0 - BETA_ONE) * grad
    second_new = BETA_TWO * second + (1.0 - BETA_TWO) * grad * grad
    fix_one = 1.0 - BETA_ONE**STEP
    fix_two = 1.0 - BETA_TWO**STEP
    step_size = first_new / fix_one / (jnp.sqrt(second_new / fix_two) + ADAM_EPS)
    return (weight - RATE * (step_size + DECAY * weight), first_new, second_new)


def body(
    input_token_ids,
    lengths,
    masked_positions,
    masked_token_targets,
    labels,
    token_embedding_table,
    position_table,
    norm_gain_table,
    query_key_value_weight,
    output_weight,
    up_weight,
    down_weight,
    adapter_inputs,
    adapter_down_input,
    head_dense_maps,
    adapter_outputs,
    class_projection,
    adapter_moment_first,
    adapter_moment_second,
    class_moment_first,
    class_moment_second,
):
    table_rows, width = token_embedding_table.shape
    seq_len = input_token_ids.shape[2]
    slots = masked_positions.shape[2]
    vocab_size = lax.axis_size("vocab")
    vocab_index = lax.axis_index("vocab")
    vocab_start = vocab_index * table_rows
    count = input_token_ids.shape[0] * input_token_ids.shape[1]
    picks = -(-(slots + 1) // 16) * 16

    packed = jnp.concatenate(
        [
            input_token_ids.reshape(count, seq_len),
            masked_positions.reshape(count, slots),
            masked_token_targets.reshape(count, slots),
            lengths.reshape(count, 1),
            labels.reshape(count, 1),
        ],
        1,
    )
    items = lax.all_gather(packed, "vocab", axis=0, tiled=True)
    item_count = items.shape[0]
    item_lengths = items[:, -2]
    number = jnp.arange(item_count)
    before = (item_lengths[None, :] > item_lengths[:, None]) | (
        (item_lengths[None, :] == item_lengths[:, None]) & (number[None, :] < number[:, None])
    )
    rank = jnp.sum(before.astype(jnp.int32), 1)
    place = rank.reshape(item_count, 1) == number[None, :]
    items = jnp.sum(jnp.where(place[:, :, None], items[:, None, :], 0), 0)
    items = items.reshape(count, vocab_size, -1)
    items = jnp.stack([items[i] if i % 2 == 0 else items[i, ::-1] for i in range(count)])
    own = lax.dynamic_index_in_dim(items, vocab_index, 1, keepdims=False)
    own_lengths, own_labels = own[:, -2], own[:, -1]
    own_positions = own[:, seq_len : seq_len + slots]

    def lookup(ids):
        local = ids - vocab_start
        inside = (local >= 0) & (local < table_rows)
        rows = jnp.take(token_embedding_table, jnp.clip(local, 0, table_rows - 1), axis=0)
        return deliver(jnp.where(inside[..., None], rows, jnp.zeros((), BF)))

    a_all, a_down, b_all = adapter_tables(adapter_inputs, adapter_down_input, adapter_outputs)
    weights = [
        (query_key_value_weight[i], output_weight[i], up_weight[i], down_weight[i], a_all[i], a_down[i], b_all[i])
        for i in range(2)
    ]
    hidden, saved0, final, saved1 = [], [], [], []
    for i in range(count):
        rows = lookup(items[i, :, :seq_len])
        out, saved = first_layer(
            own_lengths[i], rows, position_table, norm_gain_table[0], norm_gain_table[1:3], weights[0]
        )
        hidden.append(out)
        saved0.append(saved)
    target_rows = jnp.stack(
        [lookup(items[i, :, seq_len + slots : seq_len + 2 * slots]) for i in range(count)]
    )
    pick_index = jnp.concatenate(
        [own_positions, jnp.zeros((count, 1), jnp.int32), jnp.full((count, picks - slots - 1), -1, jnp.int32)], 1
    )
    for i in range(count):
        out, saved = last_layer(
            own_lengths[i], hidden[i][0], hidden[i][1], pick_index[i], norm_gain_table[3:5], weights[1]
        )
        final.append(out)
        saved1.append(saved)

    features = jnp.concatenate([f[:slots] for f in final])
    pre = dot(features, head_dense_maps[0])
    act, act_slope = gelu_both(pre)
    hat, rstd = norm_parts(act)
    gain = norm_gain_table[5]
    z = (hat * gain).astype(BF)
    z_all = lax.all_gather(z, "vocab", axis=0, tiled=True)
    summed, top, total = table_pass(z_all, token_embedding_table)
    own_slots = count * slots
    stats = lax.all_gather(jnp.concatenate([top, total], 1), "vocab", axis=0)
    top_all = jnp.max(stats[:, :, 0], 0)
    total_all = jnp.sum(stats[:, :, 1] * jnp.exp(stats[:, :, 0] - top_all), 0)
    share = total[:, 0] * jnp.exp(top[:, 0] - top_all) / total_all
    grad_z = deliver((summed * share[:, None]).astype(BF).reshape(vocab_size, own_slots, width))
    log_total = lax.dynamic_slice_in_dim(top_all + jnp.log(total_all), vocab_index * own_slots, own_slots)
    target_rows = target_rows.reshape(own_slots, width).astype(F32)
    target_logit = jnp.sum(z.astype(F32) * target_rows, -1)
    live = (jnp.arange(slots)[None, :] < own_lengths[:, None] * 15 // 100).reshape(-1)
    masked_loss = jnp.sum(jnp.where(live, log_total - target_logit, 0.0))
    grad_z = jnp.where(live[:, None], grad_z.astype(F32) - target_rows, 0.0)
    grad_pre = (norm_back(grad_z * gain, hat, rstd) * act_slope).astype(BF)
    grad_rows = dot_nt(grad_pre, head_dense_maps[0]).reshape(count, slots, width)

    first_rows = jnp.concatenate([f[slots : slots + 1] for f in final])
    pooled = jnp.tanh(dot(first_rows, head_dense_maps[1]))
    classes = class_projection.shape[1]
    class_logits = (
        jnp.sum(pooled[:, :, None] * class_projection[None, :-1, :], 1) + class_projection[-1:]
    )
    class_top = jnp.max(class_logits, -1, keepdims=True)
    class_exp = jnp.exp(class_logits - class_top)
    class_sum = jnp.sum(class_exp, -1, keepdims=True)
    label_hot = (jnp.arange(classes)[None, :] == own_labels[:, None]).astype(F32)
    class_loss = jnp.sum(class_top[:, 0] + jnp.log(class_sum[:, 0]) - jnp.sum(class_logits * label_hot, -1))
    grad_class = class_exp / class_sum - label_hot
    grad_head = jnp.concatenate(
        [
            jnp.sum(pooled[:, :, None] * grad_class[:, None, :], 0),
            jnp.sum(grad_class, 0, keepdims=True),
        ],
        0,
    )
    grad_pooled = jnp.sum(grad_class[:, None, :] * class_projection[None, :-1, :], -1)
    grad_pre_class = (grad_pooled * (1.0 - pooled * pooled)).astype(BF)
    grad_first = dot_nt(grad_pre_class, head_dense_maps[1])

    grads = [0.0, 0.0]
    for i in range(count):
        grad = jnp.concatenate(
            [grad_rows[i], grad_first[i : i + 1], jnp.zeros((picks - slots - 1, width), F32)]
        )
        grad, b_grad = last_back(own_lengths[i], grad, saved1[i], weights[1], norm_gain_table[3:5])
        grads[1] = grads[1] + b_grad
        grads[0] = grads[0] + first_back(own_lengths[i], grad, saved0[i], weights[0], norm_gain_table[1:3])

    terms = (jnp.sum(live.astype(jnp.int32)) + count).astype(F32)
    flat = jnp.concatenate(
        [
            jnp.stack(grads).reshape(-1),
            grad_head.reshape(-1),
            jnp.stack([masked_loss + class_loss, terms]),
        ]
    )
    size = flat.shape[0]
    flat = jnp.pad(flat, (0, -size % 128)).reshape(-1, 128)
    flat = reduce_all(flat).reshape(-1)
    sum_stats = flat[size - 2 : size]
    split = adapter_outputs.size
    adapter_grad = flat[:split].reshape(adapter_outputs.shape) / sum_stats[1]
    grad_head = flat[split : size - 2].reshape(class_projection.shape) / sum_stats[1]
    overall_norm = jnp.sqrt(jnp.sum(adapter_grad * adapter_grad) + jnp.sum(grad_head * grad_head))
    multiplier = CLIP_AT / jnp.maximum(overall_norm, CLIP_AT)
    adapter_new = moment_update(
        adapter_outputs, adapter_grad * multiplier, adapter_moment_first, adapter_moment_second
    )
    class_new = moment_update(
        class_projection, grad_head * multiplier, class_moment_first, class_moment_second
    )
    return (sum_stats, overall_norm.reshape(1)) + adapter_new + class_new


def solution(mesh):
    split = P(None, ("dp", "vocab"), None)
    placed = (split, P(None, ("dp", "vocab")), split, split, P(None, ("dp", "vocab")), P("vocab", None)) + (P(),) * 15
    return jax.shard_map(body, mesh=mesh, in_specs=placed, out_specs=(P(),) * 8, check_vma=False)
```

time: 964 us -> 724 us (0.75)
  blocking collectives: 111 us -> 19.8 us
  other arithmetic: 129 us -> 81.6 us
  waiting for transfers between devices: 104 us -> 57.4 us
  matrix products: 409 us -> 365 us
  between operations: 27.6 us -> 10 us
  starting transfers between devices: 5.55 us -> 22.7 us
  local copies, waits for them, and re-layouts: 168 us -> 156 us
    psum x1 -> x0, waiting for transfers between devices: 84.5 us -> none  [body(): lax.psum((adapter_out_gradient, grad_head, stats), ('dp', 'vocab'))]
    ppermute x0 -> x20, waiting for transfers between devices: none -> 57.4 us  [swap(): return lax.ppermute(value, axis, [(i, i ^ mask) for i in range(size)])]
    mul x8 -> x3, local copies, waits for them, and re-layouts: 49.2 us -> 0.54 us  [the longest x2 0.44 us: body(): grad_head * multiplier]
    psum x2 -> x0, blocking collectives: 46.6 us -> none  [the longest x1 39.7 us: body(): lax.psum((adapter_out_gradient, grad_head, stats), ('dp', 'vocab'))]
    dot_general x146 -> x148, matrix products: 409 us -> 365 us  [the longest x35 155 us: dot_nt(): lax.dot_general(left, right, (((1,), (1,)), ((), ())), preferred_element_...]
    slice x10 -> x27, local copies, waits for them, and re-layouts: 3.14 us -> 42 us  [the longest x8 28.7 us: first_layer(): q, k, v = (qkv[:, i * width:(i + 1) * width] for i in range(3))]
    ppermute x0 -> x20, starting transfers between devices: none -> 22.7 us  [swap(): return lax.ppermute(value, axis, [(i, i ^ mask) for i in range(size)])]
    gather x2 -> x6, local copies, waits for them, and re-layouts: 36.5 us -> 58 us  [lookup(): jnp.take(token_embedding_table, jnp.clip(local, 0, table_rows - 1), axis=0)]
  transfers between devices with their start and end apart: 5 -> 20, of which waited for: 2 -> 12; matrix products, arithmetic and copies ran while one was open for 5% -> 12% of each run, Pallas kernels for 0% -> 0%
where the time goes in v1:
time: 724 us; the launch traced here: 712 us
  matrix products  365 us (50%)
  local copies, waits for them, and re-layouts  156 us (22%)
  other arithmetic  81.6 us (11%)
  waiting for transfers between devices  57.4 us (8%)
  starting transfers between devices  22.7 us (3%)
  blocking collectives  19.8 us (3%)
  between operations  10 us (1%)
    dot_general x35, matrix products, dot_nt(): lax.dot_general(left, right, (((1,), (1,)), ((), ())), preferred_element_...  155 us
    dot_general x61, matrix products, dot(): return jnp.dot(left, right, preferred_element_type=F32)  115 us
    gather x6, local copies, waits for them, and re-layouts, lookup(): jnp.take(token_embedding_table, jnp.clip(local, 0, table_rows - 1), axis=0)  58 us
    ppermute x20, waiting for transfers between devices, swap(): return lax.ppermute(value, axis, [(i, i ^ mask) for i in range(size)])  57.4 us
    dot_general x28, matrix products, dot_tn(): lax.dot_general(left, right, (((0,), (0,)), ((), ())), preferred_element_...  34.2 us
    unnamed x616, local copies, waits for them, and re-layouts  31.4 us
    slice x8, local copies, waits for them, and re-layouts, first_layer(): q, k, v = (qkv[:, i * width:(i + 1) * width] for i in range(3))  28.7 us
    ppermute x20, starting transfers between devices, swap(): return lax.ppermute(value, axis, [(i, i ^ mask) for i in range(size)])  22.7 us
  transfers between devices with their start and end apart: 20, of which 12 were waited for; matrix products, arithmetic and copies ran while one was open for 12% of the time, Pallas kernels for 0%

profile of v1, /device:TPU:0, one launch (start us, length us, event | category | flops | bytes accessed | tf_op | source)
XLA Modules:
  0.0 712.2 jit_solution(15672758172423971701)
XLA Ops:
  10.8 11.4 %gather_fusion.2 = bf16[304,768]{1,0:T(8,128)(2,1)S(1)} fusion(bf16[12576,768]{1,0:T(8,128)(2,1)} %param.30, s32[1024]{0:T(1024)S(1)} %pad_clamp_fusion.1), kind=kCustom, calls=%fused_computation.1.clone | custom fusion | bytes 935104 | tf_op jit(solution)/shard_map/jit(_take)/gather | solution.py:330
  24.4 11.4 %gather_fusion.3 = bf16[304,768]{1,0:T(8,128)(2,1)S(1)} fusion(bf16[12576,768]{1,0:T(8,128)(2,1)} %param.30, s32[1024]{0:T(1024)S(1)} %pad_clamp_fusion), kind=kCustom, calls=%fused_computation.3.clone | custom fusion | bytes 935104 | tf_op jit(solution)/shard_map/jit(_take)/gather | solution.py:330
  37.3 17.4 %gather_fusion.1 = bf16[2048,768]{1,0:T(8,128)(2,1)S(1)} fusion(bf16[12576,768]{1,0:T(8,128)(2,1)} %param.30, s32[2048]{0:T(1024)S(1)} %broadcast_clamp_fusion), kind=kCustom, calls=%fused_computation.2.clone | custom fusion | bytes 6299648 | tf_op jit(solution)/shard_map/jit(_take)/gather | solution.py:330
  59.3 17.4 %gather_fusion = bf16[2048,768]{1,0:T(8,128)(2,1)S(1)} fusion(bf16[12576,768]{1,0:T(8,128)(2,1)} %param.30, s32[2048]{0:T(1024)S(1)} %broadcast_clamp_fusion.1), kind=kCustom, calls=%fused_computation.clone | custom fusion | bytes 6299648 | tf_op jit(solution)/shard_map/jit(_take)/gather | solution.py:330
  113.3 32.8 %collective-permute-done.9 = bf16[76,768]{1,0:T(8,128)(2,1)S(1)} collective-permute-done((bf16[76,768]{1,0:T(8,128)(2,1)S(1)}, bf16[76,768]{1,0:T(8,128)(2,1)S(1)}, u32[]{:S(2)}, u32[]{:S(2)}) %collective-permute-start.9) | collective-permute-done | bytes 116768 | tf_op jit(solution)/shard_map/ppermute | solution.py:62
  177.6 14.0 %copy.324 = bf16[512,768]{0,1:T(8,128)(2,1)} copy(bf16[512,768]{1,0:T(8,128)(2,1)} %get-tuple-element.111) | data formatting | bytes 1572864 | tf_op jit(solution)/shard_map/slice | solution.py:206
  236.8 8.3 %fusion.38 = f32[512,768]{1,0:T(8,128)S(1)} fusion(bf16[2,3072,768]{2,1,0:T(8,128)(2,1)} %param.36, f32[512,3072]{1,0:T(8,128)S(1)} %convolution_add_fusion.2), kind=kOutput, calls=%fused_computation.67 | convolution fusion | flops 2430074880 | bytes 12582912 | tf_op jit(solution)/shard_map/dot_general | solution.py:22
  246.1 8.3 %fusion.40 = f32[512,768]{1,0:T(8,128)S(1)} fusion(bf16[2,3072,768]{2,1,0:T(8,128)(2,1)} %param.36, f32[512,3072]{1,0:T(8,128)S(1)} %convolution_add_fusion.3), kind=kOutput, calls=%fused_computation.69 | convolution fusion | flops 2430074880 | bytes 12582912 | tf_op jit(solution)/shard_map/dot_general | solution.py:22
  326.1 8.4 %all_gather.13 = bf16[608,768]{1,0:T(8,128)(2,1)S(1)} all-gather(bf16[152,768]{1,0:T(8,128)(2,1)S(1)} %get-tuple-element.93), channel_id=1, replica_groups=mesh['dp'=8,'vocab'=4] {'vocab'}, dimensions={0}, use_global_device_ids=true | all-gather | bytes 1167360 | tf_op jit(solution)/shard_map/all_gather | solution.py:365
  334.5 22.8 %fusion.495 = (f32[608]{0:T(1024)S(1)}, f32[608,12576]{1,0:T(8,128)}) fusion(bf16[608,768]{1,0:T(8,128)(2,1)S(1)} %all_gather.13, bf16[12576,768]{1,0:T(8,128)(2,1)} %param.30), kind=kOutput, calls=%fused_computation.797 | convolution fusion | flops 11752220672 | bytes 50837888 | tf_op jit(solution)/shard_map/dot_general | solution.py:26
  357.3 13.0 %fusion = f32[608]{0:T(1024)S(1)} fusion(f32[608,12576]{1,0:T(8,128)} %get-tuple-element.179, f32[608]{0:T(1024)S(1)} %get-tuple-element.178), kind=kLoop, calls=%fused_computation.5 | loop fusion | flops 15291808 | bytes 30589696 | tf_op jit(solution)/shard_map/reduce_sum | solution.py:256
  375.7 23.3 %multiply_convert_fusion.8 = bf16[608,768]{1,0:T(8,128)(2,1)S(1)} fusion(bf16[12576,768]{1,0:T(8,128)(2,1)} %param.30, f32[608,12576]{1,0:T(8,128)} %get-tuple-element.179, f32[608]{0:T(1024)S(1)} %get-tuple-element.178, f32[608]{0:T(1024)S(1)} %get-tuple-element.133, f32[608]{0:T(1024)S(1)} %fusion), kind=kOutput, calls=%fused_computation.144 | convolution fusion | flops 11761268736 | bytes 50842752 | tf_op jit(solution)/shard_map/dot_general | solution.py:22
  505.2 6.9 fusion.36
  513.1 9.4 %multiply_convert_fusion.3 = bf16[512,3072]{1,0:T(8,128)(2,1)} fusion(f32[512,3072]{1,0:T(8,128)} %fusion.36, bf16[3072,128]{0,1:T(8,128)(2,1)} %fusion.220, f32[512,3072]{1,0:T(8,128)} %copy-done.64, bf16[512,768]{1,0:T(8,128)(2,1)S(1)} %fusion.218, bf16[128,6912]{1,0:T(8,128)(2,1)} %copy-done.12), kind=kOutput, calls=%fused_computation.32 | convolution fusion | flops 536412160 | bytes 17498112 | tf_op jit(solution)/shard_map/dot_general | solution.py:26
  532.2 6.9 fusion.463
  556.0 7.0 fusion.34
  564.0 9.1 %multiply_convert_fusion.2 = bf16[512,3072]{1,0:T(8,128)(2,1)} fusion(f32[512,3072]{1,0:T(8,128)} %fusion.34, bf16[3072,128]{0,1:T(8,128)(2,1)} %fusion.220, f32[512,3072]{1,0:T(8,128)} %copy-done.63, bf16[512,768]{1,0:T(8,128)(2,1)S(1)} %fusion.217, bf16[128,6912]{1,0:T(8,128)(2,1)S(1)} %copy-done.13), kind=kOutput, calls=%fused_computation.29 | convolution fusion | flops 536412160 | bytes 17498112 | tf_op jit(solution)/shard_map/dot_general | solution.py:26
  582.7 6.6 fusion.461
  599.8 6.8 fusion.137
  606.6 8.9 %multiply_reduce_fusion = (f32[12,512]{1,0:T(8,128)S(1)}, f32[12,512,512]{1,2,0:T(8,128)}) fusion(f32[12,512,512]{1,2,0:T(8,128)} %copy-done.1, f32[12,512]{1,0:T(8,128)S(1)} %copy-done.134, bf16[512,12,64]{0,2,1:T(8,128)(2,1)S(1)} %bitcast.556, bf16[512,12,64]{0,2,1:T(8,128)(2,1)S(1)} %bitcast.573), kind=kOutput, calls=%fused_computation.10 | convolution fusion | flops 412084224 | bytes 26787840 | tf_op jit(solution)/shard_map/qhd,khd->hqk/dot_general | solution.py:144
  615.6 7.1 multiply_convert_fusion
  630.2 6.8 fusion.134
  637.0 8.9 %multiply_reduce_fusion.1 = (f32[12,512]{1,0:T(8,128)S(1)}, f32[12,512,512]{1,2,0:T(8,128)}) fusion(f32[12,512,512]{1,2,0:T(8,128)} %copy-done, f32[12,512]{1,0:T(8,128)S(1)} %copy-done.133, bf16[512,12,64]{0,2,1:T(8,128)(2,1)S(1)} %bitcast.558, bf16[512,12,64]{0,2,1:T(8,128)(2,1)S(1)} %bitcast.571), kind=kOutput, calls=%fused_computation.13 | convolution fusion | flops 412084224 | bytes 26787840 | tf_op jit(solution)/shard_map/qhd,khd->hqk/dot_general | solution.py:144
  645.9 6.9 multiply_convert_fusion.1
  (1027 shorter events, 422.3 us)
Async XLA Ops:
  24.0 76.6 %collective-permute-start.6 = (bf16[2,76,768]{2,1,0:T(8,128)(2,1)}, bf16[2,76,768]{2,1,0:T(8,128)(2,1)}, u32[]{:S(2)}, u32[]{:S(2)}) collective-permute-start(bf16[2,76,768]{2,1,0:T(8,128)(2,1)} %dynamic-slice_bitcast_fusion.6), channel_id=1, source_target_pairs={{0,1},{1,0},{2,3},{3,2},{4,5},{5,4},{6,7},{7,6},{8,9},{9,8},{10,11... | collective-permute-start | bytes 700424 | tf_op jit(solution)/shard_map/ppermute | solution.py:62
  37.0 75.2 %collective-permute-start.8 = (bf16[2,76,768]{2,1,0:T(8,128)(2,1)}, bf16[2,76,768]{2,1,0:T(8,128)(2,1)}, u32[]{:S(2)}, u32[]{:S(2)}) collective-permute-start(bf16[2,76,768]{2,1,0:T(8,128)(2,1)} %dynamic-slice_bitcast_fusion.5), channel_id=1, source_target_pairs={{0,1},{1,0},{2,3},{3,2},{4,5},{5,4},{6,7},{7,6},{8,9},{9,8},{10,11... | collective-permute-start | bytes 700424 | tf_op jit(solution)/shard_map/ppermute | solution.py:62
  59.0 44.8 %collective-permute-start.2 = (bf16[2,512,768]{2,1,0:T(8,128)(2,1)}, bf16[2,512,768]{2,1,0:T(8,128)(2,1)}, u32[]{:S(2)}, u32[]{:S(2)}) collective-permute-start(bf16[2,512,768]{2,1,0:T(8,128)(2,1)} %dynamic-slice_bitcast_fusion), channel_id=1, source_target_pairs={{0,1},{1,0},{2,3},{3,2},{4,5},{5,4},{6,7},{7,6},{8,9},{9,8},{10,11... | collective-permute-start | bytes 4718600 | tf_op jit(solution)/shard_map/ppermute | solution.py:62
  80.7 26.4 %collective-permute-start = (bf16[2,512,768]{2,1,0:T(8,128)(2,1)}, bf16[2,512,768]{2,1,0:T(8,128)(2,1)}, u32[]{:S(2)}, u32[]{:S(2)}) collective-permute-start(bf16[2,512,768]{2,1,0:T(8,128)(2,1)} %dynamic-slice_bitcast_fusion.1), channel_id=1, source_target_pairs={{0,1},{1,0},{2,3},{3,2},{4,5},{5,4},{6,7},{7,6},{8,9},{9,8},{10,11... | collective-permute-start | bytes 4718600 | tf_op jit(solution)/shard_map/ppermute | solution.py:62
  85.5 175.4 %copy-start.154 = (f32[768]{0:T(1024)}, f32[768]{0:T(1024)S(1)}, u32[]{:S(2)}) copy-start(f32[768]{0:T(1024)S(1)} %get-tuple-element.75) | copy-start | bytes 9220
  85.6 182.5 %copy-start.190 = (f32[768]{0:T(1024)}, f32[768]{0:T(1024)S(1)}, u32[]{:S(2)}) copy-start(f32[768]{0:T(1024)S(1)} %get-tuple-element.74) | copy-start | bytes 9220
  85.6 227.0 %copy-start.164 = (f32[768]{0:T(1024)}, f32[768]{0:T(1024)S(1)}, u32[]{:S(2)}) copy-start(f32[768]{0:T(1024)S(1)} %get-tuple-element.73) | copy-start | bytes 9220
  89.9 188.2 %copy-start.8 = (bf16[128,6912]{1,0:T(8,128)(2,1)}, bf16[128,6912]{1,0:T(8,128)(2,1)S(1)}, u32[]{:S(2)}) copy-start(bf16[128,6912]{1,0:T(8,128)(2,1)S(1)} %get-tuple-element.109) | copy-start | bytes 5308420
  101.7 11.6 %collective-permute-start.7 = (bf16[76,768]{1,0:T(8,128)(2,1)S(1)}, bf16[76,768]{1,0:T(8,128)(2,1)S(1)}, u32[]{:S(2)}, u32[]{:S(2)}) collective-permute-start(bf16[76,768]{1,0:T(8,128)(2,1)S(1)} %dynamic-slice_bitcast_fusion.9), channel_id=1, source_target_pairs={{0,2},{1,3},{2,0},{3,1},{4,6},{5,7},{6,4},{7,5},{8,10},{9,11},{10,... | collective-permute-start | bytes 350216 | tf_op jit(solution)/shard_map/ppermute | solution.py:62
  107.0 41.9 %collective-permute-start.3 = (bf16[512,768]{1,0:T(8,128)(2,1)}, bf16[512,768]{1,0:T(8,128)(2,1)}, u32[]{:S(2)}, u32[]{:S(2)}) collective-permute-start(bf16[512,768]{1,0:T(8,128)(2,1)} %dynamic-slice_bitcast_fusion.2), channel_id=1, source_target_pairs={{0,2},{1,3},{2,0},{3,1},{4,6},{5,7},{6,4},{7,5},{8,10},{9,11},{10,... | collective-permute-start | bytes 2359304 | tf_op jit(solution)/shard_map/ppermute | solution.py:62
  110.2 38.7 %collective-permute-start.1 = (bf16[512,768]{1,0:T(8,128)(2,1)}, bf16[512,768]{1,0:T(8,128)(2,1)}, u32[]{:S(2)}, u32[]{:S(2)}) collective-permute-start(bf16[512,768]{1,0:T(8,128)(2,1)} %dynamic-slice_bitcast_fusion.3), channel_id=1, source_target_pairs={{0,2},{1,3},{2,0},{3,1},{4,6},{5,7},{6,4},{7,5},{8,10},{9,11},{10,... | collective-permute-start | bytes 2359304 | tf_op jit(solution)/shard_map/ppermute | solution.py:62
  113.1 33.0 %collective-permute-start.9 = (bf16[76,768]{1,0:T(8,128)(2,1)S(1)}, bf16[76,768]{1,0:T(8,128)(2,1)S(1)}, u32[]{:S(2)}, u32[]{:S(2)}) collective-permute-start(bf16[76,768]{1,0:T(8,128)(2,1)S(1)} %dynamic-slice_bitcast_fusion.8), channel_id=1, source_target_pairs={{0,2},{1,3},{2,0},{3,1},{4,6},{5,7},{6,4},{7,5},{8,10},{9,11},{10,... | collective-permute-start | bytes 350216 | tf_op jit(solution)/shard_map/ppermute | solution.py:62
  399.1 2.4 collective-permute-start.4
  403.0 8.1 %collective-permute-start.5 = (bf16[152,768]{1,0:T(8,128)(2,1)}, bf16[152,768]{1,0:T(8,128)(2,1)}, u32[]{:S(2)}, u32[]{:S(2)}) collective-permute-start(bf16[152,768]{1,0:T(8,128)(2,1)} %dynamic-slice_bitcast_fusion.7), channel_id=1, source_target_pairs={{0,2},{1,3},{2,0},{3,1},{4,6},{5,7},{6,4},{7,5},{8,10},{9,11},{10,... | collective-permute-start | bytes 700424 | tf_op jit(solution)/shard_map/ppermute | solution.py:62
  661.4 1.6 collective-permute-start.10
  663.1 5.6 collective-permute-start.11
  668.7 4.3 collective-permute-start.12
  673.1 4.0 collective-permute-start.13
  677.1 4.7 collective-permute-start.14
  681.8 4.6 collective-permute-start.15
  686.5 3.9 collective-permute-start.16
  690.4 4.3 collective-permute-start.17
  694.7 5.0 collective-permute-start.18
  699.8 1.6 collective-permute-start.19
  (300 other events, 1745.9 us)

commit v2 on v1

v2 whole, which is shorter than its diff:
```python
import functools

import jax
import jax.numpy as jnp
from jax import lax
from jax.experimental import pallas as pl
from jax.experimental.pallas import tpu as pltpu
from jax.sharding import PartitionSpec as P

HDIM = 64
STEP = 10
NORM_EPS = 1e-05
ADAPTER_SCALE = 2.0
NEG_FILL = -1e30
CLIP_AT = 0.001
RATE = 0.03
BETA_ONE = 0.9
BETA_TWO = 0.999
ADAM_EPS = 1e-08
DECAY = 0.01
BF = jnp.bfloat16
F32 = jnp.float32


def dot(left, right):
    return jnp.dot(left, right, preferred_element_type=F32)


def dot_nt(left, right):
    return lax.dot_general(left, right, (((1,), (1,)), ((), ())), preferred_element_type=F32)


def dot_tn(left, right):
    return lax.dot_general(left, right, (((0,), (0,)), ((), ())), preferred_element_type=F32)


def norm_parts(values):
    center = values - jnp.mean(values, -1, keepdims=True)
    spread = jnp.mean(center * center, -1, keepdims=True)
    rstd = lax.rsqrt(spread + NORM_EPS)
    return center * rstd, rstd


def norm_back(grad_hat, hat, rstd):
    first = jnp.mean(grad_hat, -1, keepdims=True)
    second = jnp.mean(grad_hat * hat, -1, keepdims=True)
    return rstd * (grad_hat - first - hat * second)


def gelu_both(values):
    root = 0.7978845608028654
    square = values * values
    bend = jnp.tanh(root * values * (1.0 + 0.044715 * square))
    half = 0.5 * (1.0 + bend)
    slope = half + 0.5 * values * (1.0 - bend * bend) * root * (1.0 + 0.134145 * square)
    return values * half, slope


def high_low(values):
    high = lax.reduce_precision(values, 8, 7)
    return high.astype(BF), (values - high).astype(BF)


def swap(value, axis, mask):
    size = lax.axis_size(axis)
    return lax.ppermute(value, axis, [(i, i ^ mask) for i in range(size)])


def deliver(parts):
    size = parts.shape[0]
    if size & (size - 1):
        return lax.psum_scatter(parts, "vocab", scatter_dimension=0, tiled=True)[0]
    index = lax.axis_index("vocab")
    core = index % 2
    pairs = parts.reshape((size // 2, 2) + parts.shape[1:])
    mine = lax.dynamic_index_in_dim(pairs, core, 1, keepdims=False)
    other = lax.dynamic_index_in_dim(pairs, 1 - core, 1, keepdims=False)
    mine = mine + swap(other, "vocab", 1)
    row = index // 2
    total = lax.dynamic_index_in_dim(mine, row, 0, keepdims=False)
    for mask in range(1, size // 2):
        sent = lax.dynamic_index_in_dim(mine, row ^ mask, 0, keepdims=False)
        total = total + swap(sent, "vocab", 2 * mask)
    return total


def reduce_all(flat):
    rows = flat.shape[0]
    steps = []
    for axis in ("vocab", "dp"):
        size = lax.axis_size(axis)
        mask = 1
        while mask < size:
            steps.append((axis, mask))
            mask *= 2
    pad = -rows % (8 << len(steps))
    now = jnp.pad(flat, ((0, pad), (0, 0)))
    for axis, mask in steps:
        bit = (lax.axis_index(axis) // mask) % 2
        half = now.shape[0] // 2
        keep = lax.dynamic_slice_in_dim(now, bit * half, half)
        send = lax.dynamic_slice_in_dim(now, (1 - bit) * half, half)
        now = keep + swap(send, axis, mask)
    for axis, mask in reversed(steps):
        bit = (lax.axis_index(axis) // mask) % 2
        got = swap(now, axis, mask)
        now = jnp.where(bit == 0, jnp.concatenate([now, got]), jnp.concatenate([got, now]))
    return now[:rows]


def adapter_tables(adapter_inputs, adapter_down_input, adapter_outputs):
    layers, width, columns = adapter_inputs.shape
    rank = adapter_down_input.shape[2]
    total = adapter_outputs.shape[2]
    one = jnp.pad(adapter_inputs, ((0, 0), (0, 0), (0, 64 - columns)))
    a_all = jnp.concatenate([one, one], 2)
    one = jnp.pad(adapter_down_input, ((0, 0), (0, 0), (columns, 64 - columns - rank)))
    a_down = jnp.concatenate([one, one], 2)
    high = lax.reduce_precision(ADAPTER_SCALE * adapter_outputs, 8, 7)
    both = jnp.stack([high, ADAPTER_SCALE * adapter_outputs - high], 1)
    column = jnp.arange(total) // width
    group = jnp.where(column < 4, column, jnp.where(column == 4, 5, 4))
    keep = jnp.arange(8)[:, None] == group[None, :]
    b_all = jnp.where(keep[None, None, :, None, :], both[:, :, None, :, :], 0.0)
    return a_all, a_down, b_all.reshape(layers, 128, total).astype(BF)


VMEM_SPEC = pl.BlockSpec(memory_space=pltpu.VMEM)
SMEM_SPEC = pl.BlockSpec(memory_space=pltpu.SMEM)
ANY_SPEC = pl.BlockSpec(memory_space=pl.ANY)
PARAMS = pltpu.CompilerParams(vmem_limit_bytes=60 * 2**20)
CHUNK = 16
EXTRA = 128


def chunked(rows, body, step=CHUNK):
    for start in range(0, rows, step):
        body(slice(start, start + step))


def lane_half():
    return lax.broadcasted_iota(jnp.int32, (1, 128), 1) < HDIM


def split_three(values):
    high = values.astype(BF)
    rest = values - high.astype(F32)
    middle = rest.astype(BF)
    return high, middle, (rest - middle.astype(F32)).astype(BF)


def lanes_of(parts):
    lane = lax.broadcasted_iota(jnp.int32, (1, 128), 1) % HDIM
    out = jnp.zeros((), BF)
    for i, part in reversed(list(enumerate(parts))):
        out = jnp.where(lane == i, part, out)
    return out


def key_extra(size, length):
    one = jnp.ones((), BF)
    mask = jnp.where(lax.broadcasted_iota(jnp.int32, (size, 1), 0) < length, 0.0, NEG_FILL)
    return lanes_of([one, one, one, jnp.broadcast_to(mask, (size, 128)).astype(BF)])


def attend_kernel(size, length, queries, q_at, k_at, v_at, out_ref, log_ref, score_ref, prob_ref):
    bias = jnp.where(lax.broadcasted_iota(jnp.int32, (1, size), 1) < length, 0.0, NEG_FILL)
    left = lane_half()

    def pair(p, carry):
        cols = pl.ds(pl.multiple_of(p * 128, 128), 128)
        q = q_at(cols) * 0.125
        k_t = k_at(cols).T
        v = v_at(cols)
        zero, one = jnp.zeros((), BF), jnp.ones((), BF)
        outs, tops = [], []
        for half in range(2):
            own = left if half == 0 else ~left
            score_ref[half] = dot(jnp.where(own, q, zero), k_t)
        for half in range(2):
            own = left if half == 0 else ~left
            top = []
            for start in range(0, queries, CHUNK):
                rows = slice(start, start + CHUNK)
                score = score_ref[half, rows, :] + bias
                highest = jnp.max(score, -1, keepdims=True)
                prob_ref[half, rows, :] = jnp.exp(score - highest).astype(BF)
                top.append(highest)
            outs.append(dot(prob_ref[half], jnp.where(own, v, one)))
            tops.append(jnp.concatenate(top, 0))
        total = pltpu.roll(jnp.where(left, outs[1], outs[0]), HDIM, 1)
        out_ref[:, cols] = (jnp.where(left, outs[0], outs[1]) / total).astype(BF)
        log_ref[:, cols] = jnp.where(left, tops[0], tops[1]) + jnp.log(total)
        return carry

    lax.fori_loop(0, log_ref.shape[1] // 128, pair, 0)


def attend_back_kernel(size, length, queries, q_at, k_at, v_at, o_at, g_at, log_ref, dq_ref, dk_ref, dv_ref,
                       score_ref, grad_ref, prob_ref, ds_ref):
    left = lane_half()
    k_extra = key_extra(size, length)
    one = jnp.ones((), BF)
    v_extra = lanes_of([one, one, one])
    across = jnp.where(
        (lax.broadcasted_iota(jnp.int32, (128, 128), 0) < HDIM) != left, 1.0, 0.0
    ).astype(BF)

    def pair(p, carry):
        cols = pl.ds(pl.multiple_of(p * 128, 128), 128)
        q = q_at(cols) * 0.125
        k, v, g = k_at(cols), v_at(cols), g_at(cols)
        logs = split_three(pltpu.roll(log_ref[:, cols], HDIM, 1))
        q_extra = lanes_of([-x for x in logs] + [one])
        product = g.astype(F32) * o_at(cols).astype(F32)
        high = product.astype(BF)
        low = (product - high.astype(F32)).astype(BF)
        g_extra = lanes_of([-x for x in split_three(dot(high, across) + dot(low, across))])
        for half in range(2):
            own = left if half == 0 else ~left
            score_ref[half] = dot_nt(jnp.where(own, k, k_extra), jnp.where(own, q, q_extra))
            grad_ref[half] = dot_nt(jnp.where(own, v, v_extra), jnp.where(own, g, g_extra))
        d_q, d_k, d_v = [], [], []
        for half in range(2):
            for start in range(0, size, CHUNK):
                rows = slice(start, start + CHUNK)
                prob = jnp.exp(score_ref[half, rows, :])
                prob_ref[half, rows, :] = prob.astype(BF)
                ds_ref[half, rows, :] = (prob * grad_ref[half, rows, :]).astype(BF)
            d_scores = ds_ref[half]
            d_v.append(dot(prob_ref[half], g))
            d_k.append(dot(d_scores, q))
            d_q.append(dot_tn(d_scores, k))
        dq_ref[:, cols] = (jnp.where(left, d_q[0], d_q[1]) * 0.125).astype(BF)
        dk_ref[:, cols] = jnp.where(left, d_k[0], d_k[1]).astype(BF)
        dv_ref[:, cols] = jnp.where(left, d_v[0], d_v[1]).astype(BF)
        return carry

    lax.fori_loop(0, log_ref.shape[1] // 128, pair, 0)


def weight_loads(hbm, width, sems, wqkv=None, wo=None, wu=None, wd=None, layer=0):
    wqkv_hbm, wo_hbm, wu_hbm, wd_hbm, ad_hbm, b_hbm = hbm
    pieces = {}
    if wqkv is not None:
        pieces["qkv"] = [
            (wqkv_hbm.at[layer], wqkv.at[:width, :]),
            (b_hbm.at[layer, :, pl.ds(0, 3 * width)], wqkv.at[width:, :]),
        ]
    if wo is not None:
        pieces["o"] = [
            (wo_hbm.at[layer], wo.at[:width, :]),
            (b_hbm.at[layer, :, pl.ds(3 * width, width)], wo.at[width:, :]),
        ]
    if wd is not None:
        pieces["down"] = [
            (wd_hbm.at[layer], wd.at[:, :width]),
            (ad_hbm.at[layer], wd.at[:, width:]),
        ]
    if wu is not None:
        pieces["up"] = [
            (wu_hbm.at[layer], wu.at[:width, :]),
            (b_hbm.at[layer, :, pl.ds(5 * width, wu.shape[1])], wu.at[width:, :]),
        ]
    loads, number = {}, 0
    for name, copies in pieces.items():
        loads[name] = []
        for source, target in copies:
            loads[name].append(pltpu.make_async_copy(source, target, sems.at[number]))
            number += 1
    return loads


def start_all(loads):
    for load in loads:
        load.start()


def wait_all(loads):
    for load in loads:
        load.wait()


def merge_inner(inner, inners):
    lane = lax.broadcasted_iota(jnp.int32, (1, 128), 1) % 64 // 8
    return jnp.where(
        lane < 3, inner, jnp.where(lane == 3, inners[0], jnp.where(lane == 4, inners[1], inners[2]))
    )


def upper_kernel(size, width, wide, gain_ref, gain, hidden, attn, x_ref, sum_ref, part, active, slope, wo, wu, wd,
                 a_ref, bd_ref, waits, hat1_ref, rstd1_ref, hat2_ref, rstd2_ref, slope_done):
    inner_o = dot(attn[:, :width], a_ref[...]).astype(BF)
    attn[:, width:] = inner_o
    waits("o")
    sum_ref[...] = dot(attn[...], wo[...])

    def middle(r):
        hat, rstd = norm_parts(hidden[r, :] + sum_ref[r, :])
        value = hat * gain_ref[gain : gain + 1, :]
        hidden[r, :] = value
        x_ref[r, :width] = value.astype(BF)
        hat1_ref[r, :] = hat.astype(BF)
        rstd1_ref[r, :] = jnp.broadcast_to(rstd, (CHUNK, 128))

    chunked(size, middle)
    inner_u = dot(x_ref[:, :width], a_ref[...]).astype(BF)
    x_ref[:, width:] = inner_u
    waits("up")
    waits("down")
    steps = wide // width

    def upper(j):
        part[j % 2] = dot(x_ref[...], wu[:, j * width : (j + 1) * width])

    total = None
    upper(0)
    for j in range(steps):
        if j + 1 < steps:
            upper(j + 1)
        cols = slice(j * width, (j + 1) * width)

        def bend(r):
            value, rise = gelu_both(part[j % 2, r, :])
            active[j % 2, r, :] = value.astype(BF)
            slope[r, cols] = rise.astype(BF)

        chunked(size, bend)
        down = dot(active[j % 2], wd[cols, :])
        if j == 0:
            sum_ref[...] = down[:, :width]
            total = down[:, width:]
        else:
            sum_ref[...] += down[:, :width]
            total = total + down[:, width:]
    slope_done()
    inner_d = total.astype(BF)
    sum_ref[...] += dot(inner_d, bd_ref[...])

    def last(r):
        hat, rstd = norm_parts(hidden[r, :] + sum_ref[r, :])
        hidden[r, :] = hat * gain_ref[gain + 1 : gain + 2, :]
        hat2_ref[r, :] = hat.astype(BF)
        rstd2_ref[r, :] = jnp.broadcast_to(rstd, (CHUNK, 128))

    chunked(size, last)
    return inner_o, inner_u, inner_d


def first_layer_kernel(
    length_ref, rows_ref, pos_ref, gain_ref, wqkv_hbm, wo_hbm, wu_hbm, wd_hbm, ad_hbm, b_hbm, a_ref, bd_ref,
    high_ref, low_ref, qkv_hbm, log_hbm, attn_hbm, inner_ref, hat1_ref, rstd1_ref, slope_hbm, hat2_ref, rstd2_ref,
    wqkv, wo, wu, wd, hidden, x_ref, qkv, log_ref, attn, sum_ref, part, active, slope, score, prob, sems,
):
    size, width = rows_ref.shape
    wide = wu.shape[1]
    hbm = (wqkv_hbm, wo_hbm, wu_hbm, wd_hbm, ad_hbm, b_hbm)
    loads = weight_loads(hbm, width, sems, wqkv, wo, wu, wd)
    for name in ("qkv", "o", "up", "down"):
        start_all(loads[name])
    def embed(r):
        hat, _ = norm_parts(rows_ref[r, :].astype(F32) + pos_ref[r, :].astype(F32))
        value = hat * gain_ref[0:1, :]
        hidden[r, :] = value
        x_ref[r, :width] = value.astype(BF)

    chunked(size, embed)
    inner = dot(x_ref[:, :width], a_ref[...]).astype(BF)
    x_ref[:, width:] = inner
    wait_all(loads["qkv"])
    for i in range(3):
        cols = slice(i * width, (i + 1) * width)
        qkv[:, cols] = dot(x_ref[...], wqkv[:, cols]).astype(BF)
    store_qkv = pltpu.make_async_copy(qkv, qkv_hbm, sems.at[8])
    store_qkv.start()
    attend_kernel(
        size, length_ref[0], size,
        lambda c: qkv[:, c],
        lambda c: qkv[:, pl.ds(c.start + width, 128)],
        lambda c: qkv[:, pl.ds(c.start + 2 * width, 128)],
        attn, log_ref, score, prob,
    )
    store_log = pltpu.make_async_copy(log_ref, log_hbm, sems.at[9])
    store_log.start()
    store_attn = pltpu.make_async_copy(attn.at[:, :width], attn_hbm, sems.at[10])
    store_attn.start()
    store_slope = pltpu.make_async_copy(slope, slope_hbm, sems.at[11])
    inners = upper_kernel(
        size, width, wide, gain_ref, 1, hidden, attn, x_ref, sum_ref, part, active, slope, wo, wu, wd, a_ref, bd_ref,
        lambda name: wait_all(loads[name]), hat1_ref, rstd1_ref, hat2_ref, rstd2_ref, store_slope.start,
    )
    inner_ref[...] = merge_inner(inner, inners)

    def last(r):
        value = hidden[r, :]
        high = value.astype(BF)
        high_ref[r, :] = high
        low_ref[r, :] = (value - high.astype(F32)).astype(BF)

    chunked(size, last)
    store_qkv.wait()
    store_log.wait()
    store_attn.wait()
    store_slope.wait()


def first_layer(length, rows, positions, gains, weights):
    wqkv, wo, wu, wd, a_all, a_down, b_all = weights
    size, width = rows.shape
    wide = wu.shape[2]
    shapes = [
        ((size, width), BF), ((size, width), BF), ((size, 3 * width), BF), ((size, width), F32), ((size, width), BF),
        ((size, 128), BF), ((size, width), BF), ((size, 128), F32), ((size, wide), BF), ((size, width), BF),
        ((size, 128), F32),
    ]
    v, a = VMEM_SPEC, ANY_SPEC
    high, low, *saved = pl.pallas_call(
        first_layer_kernel,
        out_shape=[jax.ShapeDtypeStruct(*s) for s in shapes],
        in_specs=[SMEM_SPEC, v, v, v] + [a] * 6 + [v] * 2,
        out_specs=[v, v, a, a, a, v, v, v, a, v, v],
        scratch_shapes=[
            pltpu.VMEM((width + EXTRA, 3 * width), BF), pltpu.VMEM((width + EXTRA, width), BF),
            pltpu.VMEM((width + EXTRA, wide), BF), pltpu.VMEM((wide, width + EXTRA), BF),
            pltpu.VMEM((size, width), F32), pltpu.VMEM((size, width + EXTRA), BF),
            pltpu.VMEM((size, 3 * width), BF), pltpu.VMEM((size, width), F32),
            pltpu.VMEM((size, width + EXTRA), BF), pltpu.VMEM((size, width), F32),
            pltpu.VMEM((2, size, width), F32), pltpu.VMEM((2, size, width), BF), pltpu.VMEM((size, wide), BF),
            pltpu.VMEM((2, size, size), F32), pltpu.VMEM((2, size, size), BF),
            pltpu.SemaphoreType.DMA((12,)),
        ],
        compiler_params=PARAMS,
    )(length.reshape(1), rows, positions, gains, wqkv, wo, wu, wd, a_down, b_all, a_all[0],
      b_all[0, :, 4 * width : 5 * width])
    return (high, low), tuple(saved)


def upper_back_kernel(size, width, wide, inner_t, grad_at, gain_ref, gain, hat2_ref, rstd2_ref, slope, hat1_ref, rstd1_ref,
                      wo, wu, wd, a_ref, bd_ref, out_ref, waits, grad2, x_ref, sum_ref, part, active, grad1_at):
    def second(r):
        value = norm_back(grad_at(r) * gain_ref[gain + 1 : gain + 2, :], hat2_ref[r, :].astype(F32), rstd2_ref[r, 0:1])
        grad2[r, :] = value
        x_ref[r, :width] = value.astype(BF)

    chunked(size, second)
    low = x_ref[:, :width]
    x_ref[:, width:] = dot_nt(low, bd_ref[...]).astype(BF)
    out_ref[:, 4 * width : 5 * width] = ADAPTER_SCALE * dot(inner_t[32:48], low)[8:]
    waits("down")
    waits("up")
    steps = wide // width

    def inward(j):
        part[j % 2] = dot_nt(x_ref[...], wd[j * width : (j + 1) * width, :])

    total = None
    inward(0)
    for j in range(steps):
        if j + 1 < steps:
            inward(j + 1)
        cols = slice(j * width, (j + 1) * width)

        def bend(r):
            active[j % 2, r, :] = (part[j % 2, r, :] * slope[r, cols].astype(F32)).astype(BF)

        chunked(size, bend)
        piece = dot_nt(active[j % 2], wu[:, cols])
        out_ref[:, (5 + j) * width : (6 + j) * width] = (
            ADAPTER_SCALE * dot(inner_t[32:48], active[j % 2])[:8]
        )
        if j == 0:
            sum_ref[...] = piece[:, :width]
            total = piece[:, width:]
        else:
            sum_ref[...] += piece[:, :width]
            total = total + piece[:, width:]
    sum_ref[...] += dot_nt(total.astype(BF), a_ref[...])

    def first(r):
        value = norm_back(
            (grad2[r, :] + sum_ref[r, :]) * gain_ref[gain : gain + 1, :], hat1_ref[r, :].astype(F32), rstd1_ref[r, 0:1]
        )
        x_ref[r, :width] = value.astype(BF)
        if grad1_at is not None:
            grad1_at[r, :] = value

    chunked(size, first)
    low = x_ref[:, :width]
    waits("o")
    both = dot_nt(low, wo[...])
    out_ref[:, 3 * width : 4 * width] = ADAPTER_SCALE * dot(inner_t[16:32], low)[8:]
    return (both[:, :width] + dot_nt(both[:, width:].astype(BF), a_ref[...])).astype(BF)


def first_back_kernel(
    length_ref, grad_ref, gain_ref, qkv_hbm, log_hbm, attn_hbm, inner_ref, hat1_ref, rstd1_ref, slope_hbm, hat2_ref,
    rstd2_ref, wqkv_hbm, wo_hbm, wu_hbm, wd_hbm, ad_hbm, b_hbm, a_ref, bd_ref,
    out_ref,
    wo, wu, wd, qkv, log_ref, attn, slope, grad2, x_ref, sum_ref, part, active, d_attn, dq, dk, dv, score, dscore,
    prob, ds, sems,
):
    size, width = grad_ref.shape
    wide = wu.shape[1]
    hbm = (wqkv_hbm, wo_hbm, wu_hbm, wd_hbm, ad_hbm, b_hbm)
    loads = weight_loads(hbm, width, sems, None, wo, wu, wd)
    loads["down"].append(pltpu.make_async_copy(slope_hbm, slope, sems.at[6]))
    loads["qkv"] = [
        pltpu.make_async_copy(source, target, sems.at[7 + i])
        for i, (source, target) in enumerate([(qkv_hbm, qkv), (log_hbm, log_ref), (attn_hbm, attn)])
    ]
    for name in ("down", "up", "o", "qkv"):
        start_all(loads[name])
    inner_t = inner_ref[...].T
    d_attn[...] = upper_back_kernel(
        size, width, wide, inner_t, lambda r: grad_ref[r, :], gain_ref, 1, hat2_ref, rstd2_ref, slope, hat1_ref,
        rstd1_ref, wo, wu, wd, a_ref, bd_ref, out_ref, lambda name: wait_all(loads[name]), grad2, x_ref, sum_ref,
        part, active, None,
    )
    wait_all(loads["qkv"])
    attend_back_kernel(
        size, length_ref[0], size,
        lambda c: qkv[:, c],
        lambda c: qkv[:, pl.ds(c.start + width, 128)],
        lambda c: qkv[:, pl.ds(c.start + 2 * width, 128)],
        lambda c: attn[:, c],
        lambda c: d_attn[:, c],
        log_ref, dq, dk, dv, score, dscore, prob, ds,
    )
    for i, ref in enumerate((dq, dk, dv)):
        start = 8 * i // 16 * 16
        out_ref[:, i * width : (i + 1) * width] = (
            ADAPTER_SCALE * dot(inner_t[start : start + 16], ref[...])[8 * i - start : 8 * i - start + 8]
        )


def first_back(length, grad, saved, weights, gains):
    wqkv, wo, wu, wd, a_all, a_down, b_all = weights
    qkv, log_total, attn, inner, hat1, rstd1, slope, hat2, rstd2 = saved
    size, width = grad.shape
    wide = wu.shape[2]
    v, a = VMEM_SPEC, ANY_SPEC
    low = pltpu.VMEM((size, width), BF)
    full = pltpu.VMEM((size, width), F32)
    return pl.pallas_call(
        first_back_kernel,
        out_shape=jax.ShapeDtypeStruct((8, b_all.shape[2]), F32),
        in_specs=[SMEM_SPEC, v, v, a, a, a, v, v, v, a, v, v] + [a] * 6 + [v, v],
        out_specs=v,
        scratch_shapes=[
            pltpu.VMEM((width + EXTRA, width), BF), pltpu.VMEM((width + EXTRA, wide), BF),
            pltpu.VMEM((wide, width + EXTRA), BF),
            pltpu.VMEM(qkv.shape, BF), full, low, pltpu.VMEM((size, wide), BF),
            full, pltpu.VMEM((size, width + EXTRA), BF), full, pltpu.VMEM((2, size, width), F32),
            pltpu.VMEM((2, size, width), BF), low, low, low, low,
            pltpu.VMEM((2, size, size), F32), pltpu.VMEM((2, size, size), F32),
            pltpu.VMEM((2, size, size), BF), pltpu.VMEM((2, size, size), BF),
            pltpu.SemaphoreType.DMA((10,)),
        ],
        compiler_params=PARAMS,
    )(length.reshape(1), grad, gains, qkv, log_total, attn, inner, hat1, rstd1, slope, hat2, rstd2,
      wqkv, wo, wu, wd, a_down, b_all, a_all[0], b_all[0, :, 4 * width : 5 * width])


def last_layer_kernel(
    length_ref, pick_ref, high0_ref, low0_ref, high1_ref, low1_ref, gain_ref,
    wqkv_hbm, wo_hbm, wu_hbm, wd_hbm, ad_hbm, b_hbm, map_hbm, a_ref, bd_ref,
    final_ref, z_ref, head_hat_ref, head_rstd_ref, head_slope_ref,
    q_ref, kv_hbm, log_ref, attn_out_ref, inner_ref, inner_kv_ref, hat1_ref, rstd1_ref, slope, hat2_ref, rstd2_ref,
    wqkv, wo, wu, wd, map_ref, hidden, x_ref, x_kv, kv, attn, sum_ref, part, active, score, prob, sems,
):
    count = len_items = kv.shape[0]
    size, width = high0_ref.shape
    rows = hidden.shape[0]
    picks = rows // count
    wide = wu.shape[1]
    hbm = (wqkv_hbm, wo_hbm, wu_hbm, wd_hbm, ad_hbm, b_hbm)
    loads = weight_loads(hbm, width, sems, wqkv, wo, wu, wd, 1)
    loads["map"] = [pltpu.make_async_copy(map_hbm.at[0], map_ref, sems.at[8])]
    for name in ("qkv", "o", "up", "down", "map"):
        start_all(loads[name])
    highs, lows = (high0_ref, high1_ref), (low0_ref, low1_ref)
    for i in range(count):
        r = slice(i * picks, (i + 1) * picks)
        hot = (pick_ref[r, :] == lax.broadcasted_iota(jnp.int32, (1, size), 1)).astype(BF)
        x = dot(hot, highs[i][...])
        x_ref[r, :width] = x.astype(BF)
        hidden[r, :] = x + dot(hot, lows[i][...])
        inner_kv = dot(highs[i][...], a_ref[...]).astype(BF)
        inner_kv_ref[i] = inner_kv
        x_kv[i, :, :width] = highs[i][...]
        x_kv[i, :, width:] = inner_kv
    inner = dot(x_ref[:, :width], a_ref[...]).astype(BF)
    x_ref[:, width:] = inner
    wait_all(loads["qkv"])
    q_ref[...] = dot(x_ref[...], wqkv[:, :width]).astype(BF)
    for i in range(count):
        for j in range(2):
            kv[i, :, j * width : (j + 1) * width] = dot(
                x_kv[i], wqkv[:, (j + 1) * width : (j + 2) * width]
            ).astype(BF)
    store_kv = pltpu.make_async_copy(kv, kv_hbm, sems.at[9])
    store_kv.start()
    for i in range(count):
        r = slice(i * picks, (i + 1) * picks)
        attend_kernel(
            size, length_ref[i], picks,
            lambda c: q_ref[r, c],
            lambda c: kv[i, :, c],
            lambda c: kv[i, :, pl.ds(c.start + width, 128)],
            attn.at[r], log_ref.at[r], score, prob,
        )
    attn_out_ref[...] = attn[:, :width]
    inners = upper_kernel(
        rows, width, wide, gain_ref, 3, hidden, attn, x_ref, sum_ref, part, active, slope, wo, wu, wd, a_ref, bd_ref,
        lambda name: wait_all(loads[name]), hat1_ref, rstd1_ref, hat2_ref, rstd2_ref, lambda: None,
    )
    inner_ref[...] = merge_inner(inner, inners)
    final_ref[...] = hidden[...].astype(BF)
    wait_all(loads["map"])
    sum_ref[...] = dot(final_ref[...], map_ref[...])

    def head(r):
        value, rise = gelu_both(sum_ref[r, :])
        hat, rstd = norm_parts(value)
        head_slope_ref[r, :] = rise
        head_hat_ref[r, :] = hat
        head_rstd_ref[r, :] = jnp.broadcast_to(rstd, (CHUNK, 128))
        z_ref[r, :] = (hat * gain_ref[5:6, :]).astype(BF)

    chunked(rows, head)
    store_kv.wait()


def last_layer(lengths, picks, hidden, gains, weights, maps):
    wqkv, wo, wu, wd, a_all, a_down, b_all = weights
    (high0, low0), (high1, low1) = hidden
    size, width = high0.shape
    wide = wu.shape[2]
    count = 2
    rows = picks.shape[0]
    shapes = [
        ((rows, width), BF), ((rows, width), BF), ((rows, width), F32), ((rows, 128), F32), ((rows, width), F32),
        ((rows, width), BF), ((count, size, 2 * width), BF), ((rows, width), F32), ((rows, width), BF),
        ((rows, 128), BF), ((count, size, 128), BF), ((rows, width), BF), ((rows, 128), F32), ((rows, wide), BF),
        ((rows, width), BF), ((rows, 128), F32),
    ]
    v, a = VMEM_SPEC, ANY_SPEC
    final, *saved = pl.pallas_call(
        last_layer_kernel,
        out_shape=[jax.ShapeDtypeStruct(*s) for s in shapes],
        in_specs=[SMEM_SPEC] + [v] * 6 + [a] * 7 + [v] * 2,
        out_specs=[v] * 6 + [a] + [v] * 9,
        scratch_shapes=[
            pltpu.VMEM((width + EXTRA, 3 * width), BF), pltpu.VMEM((width + EXTRA, width), BF),
            pltpu.VMEM((width + EXTRA, wide), BF), pltpu.VMEM((wide, width + EXTRA), BF),
            pltpu.VMEM((width, width), BF),
            pltpu.VMEM((rows, width), F32), pltpu.VMEM((rows, width + EXTRA), BF),
            pltpu.VMEM((count, size, width + EXTRA), BF), pltpu.VMEM((count, size, 2 * width), BF),
            pltpu.VMEM((rows, width + EXTRA), BF), pltpu.VMEM((rows, width), F32),
            pltpu.VMEM((2, rows, width), F32), pltpu.VMEM((2, rows, width), BF),
            pltpu.VMEM((2, rows // count, size), F32), pltpu.VMEM((2, rows // count, size), BF),
            pltpu.SemaphoreType.DMA((10,)),
        ],
        compiler_params=PARAMS,
    )(lengths, picks, high0, low0, high1, low1, gains, wqkv, wo, wu, wd, a_down, b_all, maps, a_all[1],
      b_all[1, :, 4 * width : 5 * width])
    return final, tuple(saved[:4]), tuple(saved[4:])


def last_back_kernel(
    length_ref, pick_ref, dz_ref, target_ref, live_ref, class_ref, gain_ref,
    z_ref, head_hat_ref, head_rstd_ref, head_slope_ref,
    q_ref, kv_hbm, log_ref, attn_ref, inner_ref, inner_kv_ref, hat1_ref, rstd1_ref, slope, hat2_ref, rstd2_ref,
    wqkv_hbm, wo_hbm, wu_hbm, wd_hbm, ad_hbm, b_hbm, map_hbm, a_ref, bd_ref,
    out0_ref, out1_ref, adapter_ref, loss_ref,
    wqkv, wo, wu, wd, map_ref, kv, grad, grad1, grad2, x_ref, sum_ref, part, active, d_attn, dq, dkv,
    score, dscore, prob, ds, sems,
):
    count, size, _ = kv.shape
    rows, width = grad.shape
    picks = rows // count
    wide = wu.shape[1]
    hbm = (wqkv_hbm, wo_hbm, wu_hbm, wd_hbm, ad_hbm, b_hbm)
    loads = weight_loads(hbm, width, sems, wqkv, wo, wu, wd, 1)
    loads["map"] = [pltpu.make_async_copy(map_hbm.at[0], map_ref, sems.at[8])]
    loads["kv"] = [pltpu.make_async_copy(kv_hbm, kv, sems.at[9])]
    for name in ("map", "down", "up", "o", "kv", "qkv"):
        start_all(loads[name])

    def head(r):
        live = live_ref[r, 0:1]
        target = target_ref[r, :].astype(F32)
        logit = jnp.sum(z_ref[r, :].astype(F32) * target, -1, keepdims=True)
        loss_ref[r, :] = jnp.broadcast_to(live * (live_ref[r, 1:2] - logit), (CHUNK, 128))
        grad_z = live * (dz_ref[r, :].astype(F32) - target)
        value = norm_back(grad_z * gain_ref[5:6, :], head_hat_ref[r, :], head_rstd_ref[r, 0:1])
        x_ref[r, :width] = (value * head_slope_ref[r, :]).astype(BF)

    chunked(rows, head)
    wait_all(loads["map"])
    grad[...] = dot_nt(x_ref[:, :width], map_ref[...]) + class_ref[...]
    inner_t = inner_ref[...].T
    d_attn[...] = upper_back_kernel(
        rows, width, wide, inner_t, lambda r: grad[r, :], gain_ref, 3, hat2_ref, rstd2_ref, slope, hat1_ref,
        rstd1_ref, wo, wu, wd, a_ref, bd_ref, adapter_ref, lambda name: wait_all(loads[name]), grad2, x_ref, sum_ref,
        part, active, grad1,
    )
    wait_all(loads["kv"])
    for i in range(count):
        r = slice(i * picks, (i + 1) * picks)
        attend_back_kernel(
            size, length_ref[i], picks,
            lambda c: q_ref[r, c],
            lambda c: kv[i, :, c],
            lambda c: kv[i, :, pl.ds(c.start + width, 128)],
            lambda c: attn_ref[r, c],
            lambda c: d_attn[r, c],
            log_ref.at[r], dq.at[r], dkv.at[i, :, :width], dkv.at[i, :, width:], score, dscore, prob, ds,
        )
    wait_all(loads["qkv"])
    both = dot_nt(dq[...], wqkv[:, :width])
    grad1[...] += both[:, :width] + dot_nt(both[:, width:].astype(BF), a_ref[...])
    adapter_ref[:, :width] = ADAPTER_SCALE * dot(inner_t[0:16], dq[...])[:8]
    total = None
    for i, out_ref in enumerate((out0_ref, out1_ref)):
        r = slice(i * picks, (i + 1) * picks)
        hot = (pick_ref[r, :] == lax.broadcasted_iota(jnp.int32, (1, size), 1)).astype(BF)
        value = grad1[r, :]
        high = value.astype(BF)
        low = (value - high.astype(F32)).astype(BF)
        both = dot_nt(dkv[i], wqkv[:, width:])
        out_ref[...] = (
            both[:, :width]
            + dot_nt(both[:, width:].astype(BF), a_ref[...])
            + dot_tn(jnp.concatenate([hot, hot], 0), jnp.concatenate([high, low], 0))
        )
        piece = dot(inner_kv_ref[i].T[0:32], dkv[i])
        total = piece if total is None else total + piece
    adapter_ref[:, width : 2 * width] = ADAPTER_SCALE * total[8:16, :width]
    adapter_ref[:, 2 * width : 3 * width] = ADAPTER_SCALE * total[16:24, width:]


def last_back(lengths, picks, dz, targets, live, class_grad, head, saved, gains, weights, maps):
    wqkv, wo, wu, wd, a_all, a_down, b_all = weights
    kv = saved[1]
    rows, width = dz.shape
    count, size, _ = kv.shape
    wide = wu.shape[2]
    v, a = VMEM_SPEC, ANY_SPEC
    low = pltpu.VMEM((rows, width), BF)
    full = pltpu.VMEM((rows, width), F32)
    return pl.pallas_call(
        last_back_kernel,
        out_shape=[
            jax.ShapeDtypeStruct((size, width), F32), jax.ShapeDtypeStruct((size, width), F32),
            jax.ShapeDtypeStruct((8, b_all.shape[2]), F32), jax.ShapeDtypeStruct((rows, 128), F32),
        ],
        in_specs=[SMEM_SPEC] + [v] * 11 + [a] + [v] * 9 + [a] * 7 + [v] * 2,
        out_specs=[v] * 4,
        scratch_shapes=[
            pltpu.VMEM((width + EXTRA, 3 * width), BF), pltpu.VMEM((width + EXTRA, width), BF),
            pltpu.VMEM((width + EXTRA, wide), BF), pltpu.VMEM((wide, width + EXTRA), BF),
            pltpu.VMEM((width, width), BF), pltpu.VMEM(kv.shape, BF),
            full, full, full, pltpu.VMEM((rows, width + EXTRA), BF), full, pltpu.VMEM((2, rows, width), F32),
            pltpu.VMEM((2, rows, width), BF), low, low, pltpu.VMEM(kv.shape, BF),
            pltpu.VMEM((2, size, rows // count), F32), pltpu.VMEM((2, size, rows // count), F32),
            pltpu.VMEM((2, size, rows // count), BF), pltpu.VMEM((2, size, rows // count), BF),
            pltpu.SemaphoreType.DMA((10,)),
        ],
        compiler_params=PARAMS,
    )(lengths, picks, dz, targets, live, class_grad, gains, *head, *saved, wqkv, wo, wu, wd, a_down, b_all, maps,
      a_all[1], b_all[1, :, 4 * width : 5 * width])


def class_kernel(row_ref, final_ref, map_ref, projection_ref, grad_ref, out_ref):
    width = final_ref.shape[1]
    classes = 3
    label = row_ref[...]
    live = label >= 0
    pooled = jnp.tanh(dot(final_ref[...], map_ref[...]))
    logits = [
        jnp.sum(pooled * projection_ref[c : c + 1, :width], -1, keepdims=True)
        + projection_ref[c : c + 1, width : width + 1]
        for c in range(classes)
    ]
    top = functools.reduce(jnp.maximum, logits)
    exponents = [jnp.exp(x - top) for x in logits]
    total = functools.reduce(jnp.add, exponents)
    loss = top + jnp.log(total)
    pulled = 0.0
    outs = []
    for c in range(classes):
        hit = (label == c).astype(F32)
        loss = loss - logits[c] * hit
        grad = jnp.where(live, exponents[c] / total - hit, 0.0)
        pulled = pulled + grad * projection_ref[c : c + 1, :width]
        outs.append((jnp.sum(pooled * grad, 0, keepdims=True), jnp.sum(grad, 0, keepdims=True)))
    grad_ref[...] = dot_nt((pulled * (1.0 - pooled * pooled)).astype(BF), map_ref[...])
    out_ref[...] = jnp.zeros(out_ref.shape, F32)
    for c in range(classes):
        out_ref[c : c + 1, :width] = outs[c][0]
        out_ref[c : c + 1, width:] = jnp.broadcast_to(outs[c][1], (1, 128))
    out_ref[classes : classes + 1, width:] = jnp.broadcast_to(
        jnp.sum(jnp.where(live, loss, 0.0), 0, keepdims=True), (1, 128)
    )


def class_head(rows, final, maps, projection):
    width = final.shape[1]
    turned = jnp.pad(projection.T, ((0, 8 - projection.shape[1]), (0, EXTRA - 1)))
    return pl.pallas_call(
        class_kernel,
        out_shape=[jax.ShapeDtypeStruct(final.shape, F32), jax.ShapeDtypeStruct((8, width + EXTRA), F32)],
        in_specs=[VMEM_SPEC] * 4,
        out_specs=[VMEM_SPEC] * 2,
        compiler_params=PARAMS,
    )(rows, final, maps[1], turned)


BLOCK = 1024


def table_kernel(z_ref, table_hbm, acc_ref, stat_ref, table, acc, score, prob, top, total, sems):
    rows = z_ref.shape[0]
    length = table.shape[0]
    blocks = length // BLOCK // 2 * 2
    tail = length - blocks * BLOCK
    loads = [
        pltpu.make_async_copy(
            table_hbm.at[pl.ds(i * BLOCK, BLOCK), :], table.at[pl.ds(i * BLOCK, BLOCK), :], sems.at[i]
        )
        for i in range(blocks)
    ]
    if tail:
        loads.append(
            pltpu.make_async_copy(
                table_hbm.at[pl.ds(blocks * BLOCK, tail), :], table.at[pl.ds(blocks * BLOCK, tail), :],
                sems.at[blocks],
            )
        )
    start_all(loads)
    top[...] = jnp.full(top.shape, NEG_FILL, F32)
    total[...] = jnp.zeros(total.shape, F32)
    acc[...] = jnp.zeros(acc.shape, F32)
    z = z_ref[...]

    def scores(start, size, slot):
        score[slot, :, :size] = dot_nt(z, table[pl.ds(start, size), :])

    def fold(start, size, slot):
        for first in range(0, rows, CHUNK):
            r = slice(first, first + CHUNK)
            value = score[slot, r, :size]
            before = top[r, :]
            now = jnp.maximum(before, jnp.max(value, -1, keepdims=True))
            exponent = jnp.exp(value - now[:, :1])
            prob[slot, r, :size] = exponent.astype(BF)
            shrink = jnp.exp(before - now)
            total[r, :] = total[r, :] * shrink + jnp.sum(exponent, -1, keepdims=True)
            top[r, :] = now
            acc[r, :] = acc[r, :] * shrink[:, :1]
        acc[...] += dot(prob[slot, :, :size], table[pl.ds(start, size), :])

    loads[0].wait()
    scores(0, BLOCK, 0)

    def two(i, carry):
        start = pl.multiple_of(i * 2 * BLOCK, BLOCK)
        wait_block(2 * i + 1)
        scores(start + BLOCK, BLOCK, 1)
        fold(start, BLOCK, 0)

        @pl.when(i + 1 < blocks // 2)
        def _():
            wait_block(2 * i + 2)

        scores(jnp.minimum(start + 2 * BLOCK, (blocks - 1) * BLOCK), BLOCK, 0)
        fold(start + BLOCK, BLOCK, 1)
        return carry

    def wait_block(i):
        pltpu.make_async_copy(
            table_hbm.at[pl.ds(0, BLOCK), :], table.at[pl.ds(0, BLOCK), :], sems.at[i]
        ).wait()

    lax.fori_loop(0, blocks // 2, two, 0)
    if tail:
        loads[-1].wait()
        scores(blocks * BLOCK, tail, 0)
        fold(blocks * BLOCK, tail, 0)
    acc_ref[...] = acc[...] / total[:, :1]
    stat_ref[:, :128] = top[...]
    stat_ref[:, 128:] = total[...]


def table_pass(z, table):
    rows, width = z.shape
    length = table.shape[0]
    widest = max(BLOCK, length - length // BLOCK // 2 * 2 * BLOCK)
    widest += -widest % 128
    return pl.pallas_call(
        table_kernel,
        out_shape=[jax.ShapeDtypeStruct((rows, width), F32), jax.ShapeDtypeStruct((rows, 256), F32)],
        in_specs=[VMEM_SPEC, ANY_SPEC],
        out_specs=[VMEM_SPEC] * 2,
        scratch_shapes=[
            pltpu.VMEM((length, width), BF), pltpu.VMEM((rows, width), F32),
            pltpu.VMEM((2, rows, widest), F32), pltpu.VMEM((2, rows, widest), BF),
            pltpu.VMEM((rows, 128), F32), pltpu.VMEM((rows, 128), F32),
            pltpu.SemaphoreType.DMA((length // BLOCK + 1,)),
        ],
        compiler_params=PARAMS,
    )(z, table)


def moment_update(weight, grad, first, second):
    first_new = BETA_ONE * first + (1.0 - BETA_ONE) * grad
    second_new = BETA_TWO * second + (1.0 - BETA_TWO) * grad * grad
    fix_one = 1.0 - BETA_ONE**STEP
    fix_two = 1.0 - BETA_TWO**STEP
    step_size = first_new / fix_one / (jnp.sqrt(second_new / fix_two) + ADAM_EPS)
    return (weight - RATE * (step_size + DECAY * weight), first_new, second_new)


def body(
    input_token_ids,
    lengths,
    masked_positions,
    masked_token_targets,
    labels,
    token_embedding_table,
    position_table,
    norm_gain_table,
    query_key_value_weight,
    output_weight,
    up_weight,
    down_weight,
    adapter_inputs,
    adapter_down_input,
    head_dense_maps,
    adapter_outputs,
    class_projection,
    adapter_moment_first,
    adapter_moment_second,
    class_moment_first,
    class_moment_second,
):
    table_rows, width = token_embedding_table.shape
    seq_len = input_token_ids.shape[2]
    slots = masked_positions.shape[2]
    vocab_size = lax.axis_size("vocab")
    vocab_index = lax.axis_index("vocab")
    vocab_start = vocab_index * table_rows
    count = input_token_ids.shape[0] * input_token_ids.shape[1]
    picks = -(-(slots + 1) // 16) * 16
    rest = picks - slots

    own_lengths = lengths.reshape(count)
    own_labels = labels.reshape(count)
    own_positions = masked_positions.reshape(count, slots)
    packed = jnp.concatenate(
        [
            input_token_ids.reshape(count, seq_len),
            jnp.pad(masked_token_targets.reshape(count, slots), ((0, 0), (0, rest)), constant_values=-1),
        ],
        1,
    )
    items = lax.all_gather(packed, "vocab", axis=0)

    def lookup(ids):
        local = ids - vocab_start
        inside = (local >= 0) & (local < table_rows)
        rows = jnp.take(token_embedding_table, jnp.clip(local, 0, table_rows - 1), axis=0)
        return deliver(jnp.where(inside[..., None], rows, jnp.zeros((), BF)))

    a_all, a_down, b_all = adapter_tables(adapter_inputs, adapter_down_input, adapter_outputs)
    weights = (query_key_value_weight, output_weight, up_weight, down_weight, a_all, a_down, b_all)
    hidden, saved0 = [], []
    for i in range(count):
        rows = lookup(items[:, i, :seq_len])
        out, saved = first_layer(own_lengths[i], rows, position_table, norm_gain_table, weights)
        hidden.append(out)
        saved0.append(saved)
    target_rows = lookup(items[:, :, seq_len:].reshape(vocab_size, -1))
    pick_index = jnp.concatenate(
        [own_positions, jnp.zeros((count, 1), jnp.int32), jnp.full((count, rest - 1), -1, jnp.int32)], 1
    ).reshape(-1, 1)
    final, head, saved1 = last_layer(own_lengths, pick_index, hidden, norm_gain_table, weights, head_dense_maps)

    z = head[0]
    z_all = lax.all_gather(z, "vocab", axis=0, tiled=True)
    summed, stat = table_pass(z_all, token_embedding_table)
    own_slots = count * picks
    stats = lax.all_gather(jnp.stack([stat[:, 0], stat[:, 128]], 1), "vocab", axis=0)
    top_all = jnp.max(stats[:, :, 0], 0)
    total_all = jnp.sum(stats[:, :, 1] * jnp.exp(stats[:, :, 0] - top_all), 0)
    share = stat[:, 128] * jnp.exp(stat[:, 0] - top_all) / total_all
    grad_z = deliver((summed * share[:, None]).astype(BF).reshape(vocab_size, own_slots, width))
    log_total = lax.dynamic_slice_in_dim(top_all + jnp.log(total_all), vocab_index * own_slots, own_slots)
    live = jnp.arange(picks)[None, :] < own_lengths[:, None] * 15 // 100
    live = (live & (jnp.arange(picks)[None, :] < slots)).reshape(-1)
    live_columns = jnp.pad(jnp.stack([live.astype(F32), log_total], 1), ((0, 0), (0, 126)))

    label_rows = jnp.where(jnp.arange(picks)[None, :] == slots, own_labels[:, None], -1).reshape(-1, 1)
    class_grad, class_out = class_head(label_rows, final, head_dense_maps, class_projection)

    classes = class_projection.shape[1]
    out0, out1, grads1, losses = last_back(
        own_lengths, pick_index, grad_z, target_rows, live_columns, class_grad, head, saved1, norm_gain_table,
        weights, head_dense_maps,
    )
    grads0 = 0.0
    for i, grad in enumerate((out0, out1)):
        grads0 = grads0 + first_back(own_lengths[i], grad, saved0[i], weights, norm_gain_table)
    grad_head = class_out[:classes, : width + 1].T
    terms = (jnp.sum(live.astype(jnp.int32)) + count).astype(F32)
    flat = jnp.concatenate(
        [
            grads0.reshape(-1),
            grads1.reshape(-1),
            grad_head.reshape(-1),
            jnp.stack([jnp.sum(losses[:, 0]) + class_out[classes, width], terms]),
        ]
    )
    size = flat.shape[0]
    flat = jnp.pad(flat, (0, -size % 128)).reshape(-1, 128)
    flat = reduce_all(flat).reshape(-1)
    sum_stats = flat[size - 2 : size]
    split = adapter_outputs.size
    adapter_grad = flat[:split].reshape(adapter_outputs.shape) / sum_stats[1]
    grad_head = flat[split : size - 2].reshape(class_projection.shape) / sum_stats[1]
    overall_norm = jnp.sqrt(jnp.sum(adapter_grad * adapter_grad) + jnp.sum(grad_head * grad_head))
    multiplier = CLIP_AT / jnp.maximum(overall_norm, CLIP_AT)
    adapter_new = moment_update(
        adapter_outputs, adapter_grad * multiplier, adapter_moment_first, adapter_moment_second
    )
    class_new = moment_update(
        class_projection, grad_head * multiplier, class_moment_first, class_moment_second
    )
    return (sum_stats, overall_norm.reshape(1)) + adapter_new + class_new


def solution(mesh):
    split = P(None, ("dp", "vocab"), None)
    placed = (split, P(None, ("dp", "vocab")), split, split, P(None, ("dp", "vocab")), P("vocab", None)) + (P(),) * 15
    return jax.shard_map(body, mesh=mesh, in_specs=placed, out_specs=(P(),) * 8, check_vma=False)
```

time: 724 us -> 399 us (0.55); the launches traced: 712 us -> 395 us
  matrix products: 365 us -> 0 us
  Pallas kernels: 0 us -> 207 us
  local copies, waits for them, and re-layouts: 156 us -> 78.1 us
  other arithmetic: 81.6 us -> 28.2 us
  waiting for transfers between devices: 57.4 us -> 34.4 us
    dot_general x148 -> x0, matrix products: 365 us -> none  [the longest x35 155 us: dot_nt(): lax.dot_general(left, right, (((1,), (1,)), ((), ())), preferred_element_...]
    pallas_call x0 -> x8, Pallas kernels: none -> 207 us  [the longest x2 59.3 us: first_back(): pl.pallas_call(first_back_kernel, out_shape=jax.ShapeDtypeStruct((8, b_al...]
    slice x24 -> x4, local copies, waits for them, and re-layouts: 40.2 us -> 2.74 us  [the longest x3 1.54 us: body(): share = stat[:, 128] * jnp.exp(stat[:, 0] - top_all) / total_all]
    reduce_sum x27 -> x1, other arithmetic: 29.2 us -> 1.51 us  [body(): jnp.sum(losses[:, 0]) + class_out[classes, width]]
    convert_element_type x16 -> x2, other arithmetic: 23.8 us -> 0.24 us  [the longest x1 0.17 us: body(): (summed * share[:, None]).astype(BF).reshape(vocab_size, own_slots, width)]
    ppermute x20 -> x18, waiting for transfers between devices: 57.4 us -> 34.4 us  [swap(): return lax.ppermute(value, axis, [(i, i ^ mask) for i in range(size)])]
    unnamed x616 -> x65, local copies, waits for them, and re-layouts: 31.4 us -> 8.55 us
    gather x6 -> x3, local copies, waits for them, and re-layouts: 58 us -> 47.5 us  [lookup(): jnp.take(token_embedding_table, jnp.clip(local, 0, table_rows - 1), axis=0)]
  transfers between devices with their start and end apart: 20 -> 18, of which waited for: 12 -> 12; matrix products, arithmetic and copies ran while one was open for 12% -> 17% of each run, Pallas kernels for 0% -> 30%
where the time goes in v2:
time: 399 us; the launch traced here: 395 us
  Pallas kernels  207 us (52%)
  local copies, waits for them, and re-layouts  78.1 us (20%)
  waiting for transfers between devices  34.4 us (9%)
  other arithmetic  28.2 us (7%)
  blocking collectives  22.6 us (6%)
  starting transfers between devices  18.9 us (5%)
  between operations  6.23 us (2%)
    pallas_call x2, Pallas kernels, first_back(): pl.pallas_call(first_back_kernel, out_shape=jax.ShapeDtypeStruct((8, b_al...  59.3 us
    pallas_call x2, Pallas kernels, first_layer(): pl.pallas_call(first_layer_kernel, out_shape=[jax.ShapeDtypeStruct(*s) fo...  52.9 us
    gather x3, local copies, waits for them, and re-layouts, lookup(): jnp.take(token_embedding_table, jnp.clip(local, 0, table_rows - 1), axis=0)  47.5 us
    pallas_call x1, Pallas kernels, table_pass(): pl.pallas_call(table_kernel, out_shape=[jax.ShapeDtypeStruct((rows, width...  41.1 us
    ppermute x18, waiting for transfers between devices, swap(): return lax.ppermute(value, axis, [(i, i ^ mask) for i in range(size)])  34.4 us
    pallas_call x1, Pallas kernels, last_back(): pl.pallas_call(last_back_kernel, out_shape=[jax.ShapeDtypeStruct((size, w...  28.7 us
    pallas_call x1, Pallas kernels, last_layer(): pl.pallas_call(last_layer_kernel, out_shape=[jax.ShapeDtypeStruct(*s) for...  21.5 us
    ppermute x18, starting transfers between devices, swap(): return lax.ppermute(value, axis, [(i, i ^ mask) for i in range(size)])  18.9 us
  transfers between devices with their start and end apart: 18, of which 12 were waited for; matrix products, arithmetic and copies ran while one was open for 17% of the time, Pallas kernels for 30%

profile of v2, /device:TPU:0, one launch (start us, length us, event | category | flops | bytes accessed | tf_op | source)
XLA Modules:
  0.0 395.5 jit_solution(4030266555787311048)
XLA Ops:
  2.0 6.2 %all-gather.2 = s32[4,2,592]{2,1,0:T(2,128)S(1)} all-gather(s32[1,2,592]{2,1,0:T(2,128)S(1)} %fusion.18), channel_id=2, replica_groups=mesh['dp'=8,'vocab'=4] {'vocab'}, dimensions={0}, use_global_device_ids=true | all-gather | bytes 23680 | tf_op jit(solution)/shard_map/all_gather | solution.py:968
  8.4 17.6 %gather_fusion.2 = bf16[2048,768]{1,0:T(8,128)(2,1)S(1)} fusion(bf16[12576,768]{1,0:T(8,128)(2,1)} %table_hbm.1, s32[2048]{0:T(1024)S(1)} %broadcast_clamp_fusion), kind=kCustom, calls=%fused_computation.1.clone | custom fusion | bytes 6299648 | tf_op jit(solution)/shard_map/jit(_take)/gather | solution.py:973
  30.3 17.4 %gather_fusion.1 = bf16[2048,768]{1,0:T(8,128)(2,1)S(1)} fusion(bf16[12576,768]{1,0:T(8,128)(2,1)} %table_hbm.1, s32[2048]{0:T(1024)S(1)} %broadcast_clamp_fusion.1), kind=kCustom, calls=%fused_computation.clone | custom fusion | bytes 6299648 | tf_op jit(solution)/shard_map/jit(_take)/gather | solution.py:973
  52.2 12.5 %gather_fusion = bf16[640,768]{1,0:T(8,128)(2,1)S(1)} fusion(bf16[12576,768]{1,0:T(8,128)(2,1)} %table_hbm.1, s32[1024]{0:T(1024)S(1)} %pad_clamp_fusion), kind=kCustom, calls=%fused_computation.2 | custom fusion | bytes 1968640 | tf_op jit(solution)/shard_map/jit(_take)/gather | solution.py:973
  91.3 7.0 %collective-permute-done.3 = bf16[512,768]{1,0:T(8,128)(2,1)} collective-permute-done((bf16[512,768]{1,0:T(8,128)(2,1)}, bf16[512,768]{1,0:T(8,128)(2,1)}, u32[]{:S(2)}, u32[]{:S(2)}) %collective-permute-start.3) | collective-permute-done | bytes 786464 | tf_op jit(solution)/shard_map/ppermute | solution.py:66
  100.5 26.6 %shard_map.261 = (bf16[512,768]{1,0:T(8,128)(2,1)}, bf16[512,768]{1,0:T(8,128)(2,1)}, bf16[512,2304]{1,0:T(8,128)(2,1)}, f32[512,768]{1,0:T(8,128)}, bf16[512,76...) custom-call(s32[1]{0:T(128)} %bitcast.17.length_ref, ...), custom_call_target="tpu_custom_call" | custom-call | tf_op jit(solution)/shard_map/pallas_call | solution.py:417
  129.2 26.4 %shard_map.260 = (bf16[512,768]{1,0:T(8,128)(2,1)}, bf16[512,768]{1,0:T(8,128)(2,1)}, bf16[512,2304]{1,0:T(8,128)(2,1)}, f32[512,768]{1,0:T(8,128)}, bf16[512,76...) custom-call(s32[1]{0:T(128)} %bitcast.length_ref, ...), custom_call_target="tpu_custom_call" | custom-call | tf_op jit(solution)/shard_map/pallas_call | solution.py:417
  155.5 21.5 %shard_map.262 = (bf16[160,768]{1,0:T(8,128)(2,1)}, bf16[160,768]{1,0:T(8,128)(2,1)}, f32[160,768]{1,0:T(8,128)}, f32[160,128]{1,0:T(8,128)}, f32[160,768]{1,0:T...) custom-call(s32[2]{0:T(128)} %bitcast.141, ...), custom_call_target="tpu_custom_call" | custom-call | tf_op jit(solution)/shard_map/pallas_call | solution.py:648
  177.1 10.8 %all_gather.17.z_ref = bf16[640,768]{1,0:T(8,128)(2,1)} all-gather(bf16[160,768]{1,0:T(8,128)(2,1)} %get-tuple-element.59.z_ref), channel_id=1, replica_groups=mesh['dp'=8,'vocab'=4] {'vocab'}, dimensions={0}, use_global_device_ids=true | all-gather | bytes 1228800 | tf_op jit(solution)/shard_map/all_gather | solution.py:991
  187.9 41.1 %shard_map.263 = (f32[640,768]{1,0:T(8,128)}, f32[640,256]{1,0:T(8,128)}) custom-call(bf16[640,768]{1,0:T(8,128)(2,1)} %all_gather.17.z_ref, bf16[12576,768]{1,0:T(8,128)(2,1)} %table_hbm.1), custom_call_target="tpu_custom_call" | custom-call | tf_op jit(solution)/shard_map/pallas_call | solution.py:901
  230.6 5.6 %all-gather.1 = f32[2560,2]{0,1:T(2,128)S(1)} all-gather(f32[640,2]{0,1:T(2,128)S(1)} %pad_maximum_fusion.3), channel_id=3, replica_groups=mesh['dp'=8,'vocab'=4] {'vocab'}, dimensions={0}, use_global_device_ids=true | all-gather | bytes 25600 | tf_op jit(solution)/shard_map/all_gather | solution.py:994
  243.2 3.5 shard_map.264
  250.8 28.7 %shard_map.265 = (f32[512,768]{1,0:T(8,128)}, f32[512,768]{1,0:T(8,128)}, f32[8,6912]{1,0:T(8,128)}, f32[160,128]{1,0:T(8,128)}) custom-call(s32[2]{0:T(128)} %bitcast.142, s32[160,1]{1,0:T(8,128)} %reshape.339.pick_ref, bf16[160,768]{1,0:T(8,128)(2,1)} %bitcast_add_fusion.7.dz_ref, bf16[160,768]{1,0:T(8,128)(2,1)} %bitcast_add_fusion.6.target_ref, ...), custom_call_target="tpu_custom_call" | custom-call | tf_op jit(solution)/shard_map/pallas_call | solution.py:752
  281.1 29.7 %shard_map.267 = f32[8,6912]{1,0:T(8,128)} custom-call(s32[1]{0:T(128)} %bitcast.17.length_ref, f32[512,768]{1,0:T(8,128)} %get-tuple-element.88.grad_ref, f32[6,768]{1,0:T(8,128)} %gain_ref.11, bf16[512,2304]{1,0:T(8,128)(2,1)} %get-tuple-element.89.qkv_hbm, f32[512,768]{1,0:T(8,128)} %get-tuple-element.90.log_hbm, ...), custom_call_target="tpu_custom_call" | custom-call | tf_op jit(solution)/shard_map/pallas_call | solution.py:544
  310.8 29.6 %shard_map.266 = f32[8,6912]{1,0:T(8,128)} custom-call(s32[1]{0:T(128)} %bitcast.length_ref, f32[512,768]{1,0:T(8,128)} %get-tuple-element.78.grad_ref, f32[6,768]{1,0:T(8,128)} %gain_ref.11, bf16[512,2304]{1,0:T(8,128)(2,1)} %get-tuple-element.79.qkv_hbm, f32[512,768]{1,0:T(8,128)} %get-tuple-element.80.log_hbm, ...), custom_call_target="tpu_custom_call" | custom-call | tf_op jit(solution)/shard_map/pallas_call | solution.py:544
  342.7 2.1 concatenate.49
  347.4 4.8 %collective-permute-done.9 = f32[256,128]{1,0:T(8,128)S(1)} collective-permute-done((f32[256,128]{1,0:T(8,128)S(1)}, f32[256,128]{1,0:T(8,128)S(1)}, u32[]{:S(2)}, u32[]{:S(2)}) %collective-permute-start.9) | collective-permute-done | bytes 131104 | tf_op jit(solution)/shard_map/ppermute | solution.py:66
  353.8 2.8 collective-permute-done.10
  358.3 2.4 collective-permute-done.11
  360.6 2.7 collective-permute-start.12
  365.4 2.7 collective-permute-start.13
  371.6 2.4 collective-permute-done.14
  375.5 2.8 collective-permute-done.15
  379.0 4.3 %collective-permute-done.16 = f32[256,128]{1,0:T(8,128)S(1)} collective-permute-done((f32[256,128]{1,0:T(8,128)S(1)}, f32[256,128]{1,0:T(8,128)S(1)}, u32[]{:S(2)}, u32[]{:S(2)}) %collective-permute-start.16) | collective-permute-done | bytes 131104 | tf_op jit(solution)/shard_map/ppermute | solution.py:66
  (203 shorter events, 78.0 us)
Async XLA Ops:
  30.0 45.0 %collective-permute-start.2 = (bf16[2,512,768]{2,1,0:T(8,128)(2,1)}, bf16[2,512,768]{2,1,0:T(8,128)(2,1)}, u32[]{:S(2)}, u32[]{:S(2)}) collective-permute-start(bf16[2,512,768]{2,1,0:T(8,128)(2,1)} %dynamic-slice_bitcast_fusion), channel_id=1, source_target_pairs={{0,1},{1,0},{2,3},{3,2},{4,5},{5,4},{6,7},{7,6},{8,9},{9,8},{10,11... | collective-permute-start | bytes 4718600 | tf_op jit(solution)/shard_map/ppermute | solution.py:66
  51.7 27.9 %collective-permute-start = (bf16[2,512,768]{2,1,0:T(8,128)(2,1)}, bf16[2,512,768]{2,1,0:T(8,128)(2,1)}, u32[]{:S(2)}, u32[]{:S(2)}) collective-permute-start(bf16[2,512,768]{2,1,0:T(8,128)(2,1)} %dynamic-slice_bitcast_fusion.1), channel_id=1, source_target_pairs={{0,1},{1,0},{2,3},{3,2},{4,5},{5,4},{6,7},{7,6},{8,9},{9,8},{10,11... | collective-permute-start | bytes 4718600 | tf_op jit(solution)/shard_map/ppermute | solution.py:66
  66.9 19.8 %collective-permute-start.6 = (bf16[2,160,768]{2,1,0:T(8,128)(2,1)}, bf16[2,160,768]{2,1,0:T(8,128)(2,1)}, u32[]{:S(2)}, u32[]{:S(2)}) collective-permute-start(bf16[2,160,768]{2,1,0:T(8,128)(2,1)} %dynamic-slice_bitcast_fusion.4), channel_id=1, source_target_pairs={{0,1},{1,0},{2,3},{3,2},{4,5},{5,4},{6,7},{7,6},{8,9},{9,8},{10,11... | collective-permute-start | bytes 1474568 | tf_op jit(solution)/shard_map/ppermute | solution.py:66
  77.7 20.7 %collective-permute-start.3 = (bf16[512,768]{1,0:T(8,128)(2,1)}, bf16[512,768]{1,0:T(8,128)(2,1)}, u32[]{:S(2)}, u32[]{:S(2)}) collective-permute-start(bf16[512,768]{1,0:T(8,128)(2,1)} %dynamic-slice_bitcast_fusion.2), channel_id=1, source_target_pairs={{0,2},{1,3},{2,0},{3,1},{4,6},{5,7},{6,4},{7,5},{8,10},{9,11},{10,... | collective-permute-start | bytes 2359304 | tf_op jit(solution)/shard_map/ppermute | solution.py:66
  82.2 44.9 %collective-permute-start.1 = (bf16[512,768]{1,0:T(8,128)(2,1)}, bf16[512,768]{1,0:T(8,128)(2,1)}, u32[]{:S(2)}, u32[]{:S(2)}) collective-permute-start(bf16[512,768]{1,0:T(8,128)(2,1)} %dynamic-slice_bitcast_fusion.3), channel_id=1, source_target_pairs={{0,2},{1,3},{2,0},{3,1},{4,6},{5,7},{6,4},{7,5},{8,10},{9,11},{10,... | collective-permute-start | bytes 2359304 | tf_op jit(solution)/shard_map/ppermute | solution.py:66
  89.4 150.7 %collective-permute-start.7 = (bf16[160,768]{1,0:T(8,128)(2,1)}, bf16[160,768]{1,0:T(8,128)(2,1)}, u32[]{:S(2)}, u32[]{:S(2)}) collective-permute-start(bf16[160,768]{1,0:T(8,128)(2,1)} %dynamic-slice_bitcast_fusion.6), channel_id=1, source_target_pairs={{0,2},{1,3},{2,0},{3,1},{4,6},{5,7},{6,4},{7,5},{8,10},{9,11},{10,... | collective-permute-start | bytes 737288 | tf_op jit(solution)/shard_map/ppermute | solution.py:66
  236.9 5.0 %collective-permute-start.4 = (bf16[2,160,768]{2,1,0:T(8,128)(2,1)S(1)}, bf16[2,160,768]{2,1,0:T(8,128)(2,1)S(1)}, u32[]{:S(2)}, u32[]{:S(2)}) collective-permute-start(bf16[2,160,768]{2,1,0:T(8,128)(2,1)S(1)} %dynamic-slice_bitcast_fusion.5), channel_id=1, source_target_pairs={{0,1},{1,0},{2,3},{3,2},{4,5},{5,4},{6,7},{7,6},{8,9},{9,8},{10,11... | collective-permute-start | bytes 1474568 | tf_op jit(solution)/shard_map/ppermute | solution.py:66
  242.0 8.1 %collective-permute-start.5 = (bf16[160,768]{1,0:T(8,128)(2,1)S(1)}, bf16[160,768]{1,0:T(8,128)(2,1)S(1)}, u32[]{:S(2)}, u32[]{:S(2)}) collective-permute-start(bf16[160,768]{1,0:T(8,128)(2,1)S(1)} %dynamic-slice_bitcast_fusion.7), channel_id=1, source_target_pairs={{0,2},{1,3},{2,0},{3,1},{4,6},{5,7},{6,4},{7,5},{8,10},{9,11},{10,... | collective-permute-start | bytes 737288 | tf_op jit(solution)/shard_map/ppermute | solution.py:66
  310.8 29.6 %copy-start.13 = (f32[8,6912]{1,0:T(8,128)S(1)}, f32[8,6912]{1,0:T(8,128)}, u32[]{:S(2)}) copy-start(f32[8,6912]{1,0:T(8,128)} %shard_map.267) | copy-start | bytes 663556
  310.8 30.6 %copy-start.16 = (f32[8,6912]{1,0:T(8,128)S(1)}, f32[8,6912]{1,0:T(8,128)}, u32[]{:S(2)}) copy-start(f32[8,6912]{1,0:T(8,128)} %get-tuple-element.98) | copy-start | bytes 663556
  345.0 1.6 collective-permute-start.8
  346.6 5.6 %collective-permute-start.9 = (f32[256,128]{1,0:T(8,128)S(1)}, f32[256,128]{1,0:T(8,128)S(1)}, u32[]{:S(2)}, u32[]{:S(2)}) collective-permute-start(f32[256,128]{1,0:T(8,128)S(1)} %constant_dynamic-slice_fusion.3), channel_id=1, source_target_pairs={{0,2},{1,3},{2,0},{3,1},{4,6},{5,7},{6,4},{7,5},{8,10},{9,11},{10,... | collective-permute-start | bytes 393224 | tf_op jit(solution)/shard_map/ppermute | solution.py:66
  352.3 4.3 %collective-permute-start.10 = (f32[128,128]{1,0:T(8,128)S(1)}, f32[128,128]{1,0:T(8,128)S(1)}, u32[]{:S(2)}, u32[]{:S(2)}) collective-permute-start(f32[128,128]{1,0:T(8,128)S(1)} %constant_dynamic-slice_fusion.2), channel_id=1, source_target_pairs={{0,4},{4,0},{8,12},{12,8},{16,20},{20,16},{24,28},{28,24},{1,5},{5... | collective-permute-start | bytes 196616 | tf_op jit(solution)/shard_map/ppermute | solution.py:66
  356.6 4.0 %collective-permute-start.11 = (f32[64,128]{1,0:T(8,128)S(1)}, f32[64,128]{1,0:T(8,128)S(1)}, u32[]{:S(2)}, u32[]{:S(2)}) collective-permute-start(f32[64,128]{1,0:T(8,128)S(1)} %constant_dynamic-slice_fusion.1), channel_id=1, source_target_pairs={{0,8},{4,12},{8,0},{12,4},{16,24},{20,28},{24,16},{28,20},{1,9},{5... | collective-permute-start | bytes 98312 | tf_op jit(solution)/shard_map/ppermute | solution.py:66
  360.6 4.7 %collective-permute-start.12 = (f32[32,128]{1,0:T(8,128)S(1)}, f32[32,128]{1,0:T(8,128)S(1)}, u32[]{:S(2)}, u32[]{:S(2)}) collective-permute-start(f32[32,128]{1,0:T(8,128)S(1)} %constant_dynamic-slice_fusion), channel_id=1, source_target_pairs={{0,16},{4,20},{8,24},{12,28},{16,0},{20,4},{24,8},{28,12},{1,17},{... | collective-permute-start | bytes 49160 | tf_op jit(solution)/shard_map/ppermute | solution.py:66
  365.4 4.6 %collective-permute-start.13 = (f32[32,128]{1,0:T(8,128)S(1)}, f32[32,128]{1,0:T(8,128)S(1)}, u32[]{:S(2)}, u32[]{:S(2)}) collective-permute-start(f32[32,128]{1,0:T(8,128)S(1)} %dynamic-slice_add_fusion.3), channel_id=1, source_target_pairs={{0,16},{4,20},{8,24},{12,28},{16,0},{20,4},{24,8},{28,12},{1,17},{... | collective-permute-start | bytes 49160 | tf_op jit(solution)/shard_map/ppermute | solution.py:66
  370.0 3.9 collective-permute-start.14
  373.9 4.3 %collective-permute-start.15 = (f32[128,128]{1,0:T(8,128)S(1)}, f32[128,128]{1,0:T(8,128)S(1)}, u32[]{:S(2)}, u32[]{:S(2)}) collective-permute-start(f32[128,128]{1,0:T(8,128)S(1)} %maximum_select_fusion.3), channel_id=1, source_target_pairs={{0,4},{4,0},{8,12},{12,8},{16,20},{20,16},{24,28},{28,24},{1,5},{5... | collective-permute-start | bytes 196616 | tf_op jit(solution)/shard_map/ppermute | solution.py:66
  378.3 5.0 %collective-permute-start.16 = (f32[256,128]{1,0:T(8,128)S(1)}, f32[256,128]{1,0:T(8,128)S(1)}, u32[]{:S(2)}, u32[]{:S(2)}) collective-permute-start(f32[256,128]{1,0:T(8,128)S(1)} %maximum_select_fusion.2), channel_id=1, source_target_pairs={{0,2},{1,3},{2,0},{3,1},{4,6},{5,7},{6,4},{7,5},{8,10},{9,11},{10,... | collective-permute-start | bytes 393224 | tf_op jit(solution)/shard_map/ppermute | solution.py:66
  383.3 1.6 collective-permute-start.17
  383.4 8.7 %copy-start.20 = (f32[769,3]{0,1:T(4,128)S(1)}, f32[769,3]{0,1:T(4,128)}, u32[]{:S(2)}) copy-start(f32[769,3]{0,1:T(4,128)} %param.42) | copy-start | bytes 27688
  383.4 9.3 %copy-start.12 = (f32[2,8,6912]{2,1,0:T(8,128)S(1)}, f32[2,8,6912]{2,1,0:T(8,128)}, u32[]{:S(2)}) copy-start(f32[2,8,6912]{2,1,0:T(8,128)} %param.38) | copy-start | bytes 1327108
  383.4 9.3 %copy-start.14 = (f32[2,8,6912]{2,1,0:T(8,128)S(1)}, f32[2,8,6912]{2,1,0:T(8,128)}, u32[]{:S(2)}) copy-start(f32[2,8,6912]{2,1,0:T(8,128)} %param.40) | copy-start | bytes 1327108
  383.5 9.3 %copy-start.15 = (f32[2,8,6912]{2,1,0:T(8,128)S(1)}, f32[2,8,6912]{2,1,0:T(8,128)}, u32[]{:S(2)}) copy-start(f32[2,8,6912]{2,1,0:T(8,128)} %param.41) | copy-start | bytes 1327108
  (23 other events, 81.7 us)
